TPU v7x, 128 devices: a whole 4x4x4 slice. The times are simulated.
128 devices in a mesh: rep: 32 (over y_lo, x, z), tp: 4 (over y_hi, core).
Axes of the slice: x: 4, y: 4 (y_hi: 2, y_lo: 2; y = y_hi * 2 + y_lo), z: 4, core: 2. Of those that a mesh axis runs over, the one named last changes fastest.
Arguments:
- tokens: bfloat16 [14336, 5120], P('rep', 'tp'), may hold values from -6 to 6
- prompt_rows: bfloat16 [4096, 5120], P('rep', 'tp'), may hold values from -6 to 6
- norm_gain: float32 [5120], replicated, may hold values from 0.5 to 2
- w_query: float32 [5120, 4096], P(('rep', 'tp')), may hold values from -0.078125 to 0.078125
- w_key: float32 [5120, 512], P(('rep', 'tp')), may hold values from -0.078125 to 0.078125
- w_value: float32 [5120, 512], P(('rep', 'tp')), may hold values from -0.078125 to 0.078125
- w_out: float32 [4096, 5120], P(None, ('rep', 'tp')), may hold values from -0.09375 to 0.09375
- q_gain: float32 [128], replicated, may hold values from 0.5 to 2.5
- k_gain: float32 [128], replicated, may hold values from 0.5 to 2.5
- seq_lengths: int32 [4], replicated, may hold values from 1 to 224, 448 in all
- prompt_group: int32 [128], P('rep'), may hold values from 0 to 31
- prompt_blocks: int32 [128], P('rep'), may hold values from 1 to 2
- dest_offset: int32 [4], replicated, may hold values from 0 to 31
Outputs:
- returned: bfloat16 [14336, 5120], P('rep', 'tp')
Inputs may be any that keep to these rules, and one draw needn't show every extreme that they name: `seq_lengths`: the same lengths hold on every replica and sum to 448. Slot j of replica s returns to learner shard (s + dest_offset[j]) mod 32, at the same rows.
All inputs are finite; a program needn't handle non-finite values.
Results may differ from a plain program's by a relative error of at most 0.013.
Values may be sent and summed in bfloat16 or wider, within the bound.
A program may use at most 128 MiB of HBM per device.

v0:
```python
import jax
import jax.numpy as jnp
from jax import lax
from jax.sharding import PartitionSpec as P

PBLK = 64


epsilon = 1e-06
rope_base = 1000000.0


def from_behind(block, axis, distance):
    devices = range(lax.axis_size(axis))
    route = [((i - distance) % len(devices), i) for i in devices]
    return lax.ppermute(block, axis, route)


def rms_rows(values, gain_row):
    floats = values.astype(jnp.float32)
    scaled = lax.rsqrt(jnp.mean(floats * floats, axis=-1, keepdims=True) + epsilon)
    return floats * scaled * gain_row


def rotary(values, positions):
    half_size = values.shape[-1] // 2
    spread = jnp.arange(half_size, dtype=jnp.float32) * (2.0 / values.shape[-1])
    frequency = rope_base ** (-spread)
    angles = positions.astype(jnp.float32)[:, None] * frequency[None, :]
    cosine = jnp.cos(angles)[:, None, :]
    sine_part = jnp.sin(angles)[:, None, :]
    front_half = values[..., :half_size]
    back_half = values[..., half_size:]
    return jnp.concatenate(
        [front_half * cosine - back_half * sine_part, back_half * cosine + front_half * sine_part],
        axis=-1,
    )


def slot_layout(seq_lengths, row_count):
    ends_at = jnp.cumsum(seq_lengths)
    starts_at = ends_at - seq_lengths
    position = jnp.arange(row_count, dtype=jnp.int32)
    slot_of = jnp.sum((position[:, None] >= ends_at[None, :]).astype(jnp.int32), axis=1)
    onehot = (
        slot_of[:, None] == jnp.arange(seq_lengths.shape[0], dtype=jnp.int32)[None, :]
    ).astype(jnp.int32)
    within = position - jnp.sum(onehot * starts_at[None, :], axis=1)
    return (slot_of, within, onehot)


def attend(
    queries, own_keys, own_values, shared_keys, shared_values, slot_of, prefix_len, prompt_len
):
    row_count = queries.shape[0]
    head_size = queries.shape[-1]
    all_keys = jnp.concatenate([shared_keys, own_keys], axis=0)
    all_values = jnp.concatenate([shared_values, own_values], axis=0)
    shared_index = jnp.arange(shared_keys.shape[0], dtype=jnp.int32)
    shared_mask = ((shared_index // prompt_len)[None, :] == slot_of[:, None]) & (
        (shared_index % prompt_len)[None, :] < prefix_len[:, None]
    )
    position = jnp.arange(row_count, dtype=jnp.int32)
    own_mask = (slot_of[None, :] == slot_of[:, None]) & (position[None, :] <= position[:, None])
    allowed = jnp.concatenate([shared_mask, own_mask], axis=1)
    scores = jnp.einsum(
        "rkgd,nkd->kgrn", queries, all_keys, preferred_element_type=jnp.float32
    ) * head_size ** (-0.5)
    weights = jnp.where(allowed[None, None], jnp.exp(scores), 0.0)
    weighted = (weights / jnp.sum(weights, axis=-1, keepdims=True)).astype(jnp.bfloat16)
    blended = jnp.einsum("kgrn,nkd->rkgd", weighted, all_values, preferred_element_type=jnp.float32)
    return blended.reshape(row_count, -1).astype(jnp.bfloat16)


def shards(
    tokens,
    prompt_rows,
    norm_gain,
    w_query,
    w_key,
    w_value,
    w_out,
    q_gain,
    k_gain,
    seq_lengths,
    prompt_group,
    prompt_blocks,
    dest_offset,
):
    replicas = lax.axis_size("rep")
    row_count = tokens.shape[0]
    prompt_len = prompt_rows.shape[0]
    head_size = q_gain.shape[0]
    full_tokens, full_prompt = (
        lax.all_gather(tokens, "tp", axis=1, tiled=True),
        lax.all_gather(prompt_rows, "tp", axis=1, tiled=True),
    )
    normed = rms_rows(full_tokens, norm_gain).astype(jnp.bfloat16)
    prompt_normed = rms_rows(full_prompt, norm_gain).astype(jnp.bfloat16)
    combined = jnp.concatenate([normed, prompt_normed], axis=0)
    query_cols, key_cols, value_cols = (
        lax.all_to_all(w_query.astype(jnp.bfloat16), "tp", split_axis=1, concat_axis=0, tiled=True),
        lax.all_to_all(w_key.astype(jnp.bfloat16), "tp", split_axis=1, concat_axis=0, tiled=True),
        lax.all_to_all(w_value.astype(jnp.bfloat16), "tp", split_axis=1, concat_axis=0, tiled=True),
    )
    pieces = (
        lax.all_gather(query_cols, "rep", axis=0, tiled=True),
        lax.all_gather(key_cols, "rep", axis=0, tiled=True),
        lax.all_gather(value_cols, "rep", axis=0, tiled=True),
    )
    span = pieces[0].shape[0]
    query_sum = jnp.dot(combined[:row_count], pieces[0], preferred_element_type=jnp.float32)
    key_sum = jnp.dot(combined, pieces[1], preferred_element_type=jnp.float32)
    value_sum = jnp.dot(combined, pieces[2], preferred_element_type=jnp.float32)
    kv_heads = key_cols.shape[1] // head_size
    q_heads = query_cols.shape[1] // head_size
    group_size = q_heads // kv_heads
    slot_of, within, onehot = slot_layout(seq_lengths, row_count)
    prefix_len = jnp.sum(onehot * (prompt_blocks * PBLK)[None, :], axis=1)
    positions = prefix_len + within
    queries = rotary(rms_rows(query_sum.reshape(row_count, q_heads, head_size), q_gain), positions)
    queries = queries.astype(jnp.bfloat16).reshape(row_count, kv_heads, group_size, head_size)
    own_keys = rotary(
        rms_rows(key_sum[:row_count].reshape(row_count, kv_heads, head_size), k_gain), positions
    ).astype(jnp.bfloat16)
    prompt_keys = rotary(
        rms_rows(key_sum[row_count:].reshape(prompt_len, kv_heads, head_size), k_gain),
        jnp.arange(prompt_len, dtype=jnp.int32),
    ).astype(jnp.bfloat16)
    values_all = value_sum.astype(jnp.bfloat16)
    own_values = values_all[:row_count].reshape(row_count, kv_heads, head_size)
    prompt_values = values_all[row_count:]
    chooser = (prompt_group[:, None] == jnp.arange(replicas, dtype=jnp.int32)[None, :]).astype(
        jnp.bfloat16
    )
    slot_count = seq_lengths.shape[0]
    pieces = (
        lax.all_gather(prompt_keys.reshape(prompt_len, -1), "rep", axis=0, tiled=True),
        lax.all_gather(prompt_values, "rep", axis=0, tiled=True),
    )
    span = pieces[0].shape[0] // prompt_len

    def pick(piece_block):
        return jnp.einsum(
            "sm,mpc->spc",
            chooser,
            piece_block.reshape(span, prompt_len, piece_block.shape[1]),
            preferred_element_type=jnp.float32,
        )

    shared_keys = pick(pieces[0])
    shared_values = pick(pieces[1])
    shared_keys = shared_keys.astype(jnp.bfloat16).reshape(
        slot_count * prompt_len, kv_heads, head_size
    )
    shared_values = shared_values.astype(jnp.bfloat16).reshape(
        slot_count * prompt_len, kv_heads, head_size
    )
    blended = attend(
        queries, own_keys, own_values, shared_keys, shared_values, slot_of, prefix_len, prompt_len
    )
    out_rows = lax.all_to_all(
        w_out.astype(jnp.bfloat16), "tp", split_axis=0, concat_axis=1, tiled=True
    )
    partial_sum = jnp.dot(
        blended,
        lax.all_gather(out_rows, "rep", axis=1, tiled=True),
        preferred_element_type=jnp.float32,
    )
    projected = lax.psum_scatter(
        partial_sum.astype(jnp.bfloat16), "tp", scatter_dimension=1, tiled=True
    ).astype(jnp.float32)
    layer_out = (tokens.astype(jnp.float32) + projected).astype(jnp.bfloat16)
    shift_rows = jnp.sum(onehot * dest_offset[None, :], axis=1)
    current = layer_out
    for level in range(replicas.bit_length() - 1):
        moving = (shift_rows // 2**level % 2 == 1)[:, None]
        arrived = from_behind(current, "rep", 2**level)
        current = jnp.where(moving, arrived, current)
    return current


def solution(mesh):
    return jax.shard_map(
        shards,
        mesh=mesh,
        in_specs=(
            P("rep", "tp"),
            P("rep", "tp"),
            P(),
            P(("rep", "tp"), None),
            P(("rep", "tp"), None),
            P(("rep", "tp"), None),
            P(None, ("rep", "tp")),
            P(),
            P(),
            P(),
            P("rep"),
            P("rep"),
            P(),
        ),
        out_specs=P("rep", "tp"),
        check_vma=False,
    )
```

profile of v0, /device:TPU:16, one launch (start us, length us, event | category | flops | bytes accessed | tf_op | source)
XLA Modules:
  0.0 1247.9 jit_solution(16266409867261641175)
XLA Ops:
  6.5 0.7 all-gather.11.cloned.1.call-update
  7.3 0.7 all-gather.9.cloned.1.call-update
  8.1 0.9 copy_bitcast_fusion.2
  8.9 6.7 all_to_all.76
  15.7 1.5 copy_bitcast_fusion.3
  17.2 6.7 all-to-all-start
  23.9 2.5 all-to-all-done
  26.5 0.6 copy-done.5
  27.1 4.1 all-gather.11.cloned.1.call-done
  31.2 1.8 fusion.8
  33.0 0.4 fusion.10
  33.4 39.7 %all-gather.9.cloned.1.call-done = bf16[448,5120]{1,0:T(8,128)(2,1)} async-done(((bf16[448,1280]{1,0:T(8,128)(2,1)}), bf16[448,5120]{1,0:T(8,128)(2,1)}) %all-gather.9.cloned.1.call-update) | async-done | bytes 4587536 | tf_op jit(solution)/shard_map/all_gather | solution.py:95
  73.1 3.4 fusion.1
  76.5 0.2 copy-done
  76.8 3.7 fusion.3
  80.5 148.1 %all-gather.17.cloned.1.call-done = bf16[5120,128]{1,0:T(8,128)(2,1)} async-done(((bf16[160,128]{1,0:T(8,128)(2,1)}), bf16[5120,128]{1,0:T(8,128)(2,1)}) %all-gather.17.cloned.1.call-update) | async-done | bytes 1310736 | tf_op jit(solution)/shard_map/all_gather | solution.py:108
  228.6 4.4 fusion.6
  232.9 0.1 multiply_reduce_fusion.2
  233.2 0.3 fusion.51
  233.5 0.7 pad_maximum_fusion.5
  234.3 148.0 %all-gather.13.cloned.1.call-done = bf16[5120,128]{1,0:T(8,128)(2,1)} async-done(((bf16[160,128]{1,0:T(8,128)(2,1)}), bf16[5120,128]{1,0:T(8,128)(2,1)}) %all-gather.13.cloned.1.call-update) | async-done | bytes 1310736 | tf_op jit(solution)/shard_map/all_gather | solution.py:109
  382.3 4.4 fusion.18
  386.7 0.6 slice.40
  387.5 9.9 all_to_all.77
  397.5 11.3 all_to_all.78
  408.9 0.2 reduce-window.8
  409.2 0.1 select_reduce_fusion.2
  409.3 0.2 fusion.27
  409.5 0.3 compare_and_fusion
  409.9 0.9 multiply_cosine_fusion
  410.8 0.1 multiply_reduce_fusion.1
  410.9 0.7 slice_bitcast_fusion
  411.6 0.1 multiply_bitcast_fusion
  411.7 1.3 fusion.39
  413.0 122.2 %all-gather.19.cloned.1.call-done = bf16[4096,128]{1,0:T(8,128)(2,1)} async-done(((bf16[128,128]{1,0:T(8,128)(2,1)}), bf16[4096,128]{1,0:T(8,128)(2,1)}) %all-gather.19.cloned.1.call-update) | async-done | bytes 1048592 | tf_op jit(solution)/shard_map/all_gather | solution.py:138
  535.2 1.9 convolution_convert_fusion.1
  537.1 150.9 %all-gather.15.cloned.1.call-done = bf16[4096,128]{1,0:T(8,128)(2,1)} async-done(((bf16[128,128]{1,0:T(8,128)(2,1)}), bf16[4096,128]{1,0:T(8,128)(2,1)}) %all-gather.15.cloned.1.call-update) | async-done | bytes 1048592 | tf_op jit(solution)/shard_map/all_gather | solution.py:139
  688.0 1.9 convolution_convert_fusion.2
  689.9 170.6 %all-gather.21.cloned.1.call-done = bf16[5120,1024]{1,0:T(8,128)(2,1)} async-done(((bf16[160,1024]{1,0:T(8,128)(2,1)}), bf16[5120,1024]{1,0:T(8,128)(2,1)}) %all-gather.21.cloned.1.call-update) | async-done | bytes 10485776 | tf_op jit(solution)/shard_map/all_gather | solution.py:107
  860.5 9.0 fusion.83
  869.4 0.4 copy.71
  869.9 0.5 multiply_reduce_fusion
  870.4 0.1 copy.62
  870.5 0.5 fusion.11
  871.1 0.7 subtract_convert_fusion
  871.8 4.3 fusion
  876.1 4.0 fusion.15
  880.2 0.6 copy.64
  880.8 151.6 %all-gather.23.cloned.1.call-done = bf16[1024,5120]{0,1:T(8,128)(2,1)} async-done(((bf16[1024,160]{0,1:T(8,128)(2,1)}), bf16[1024,5120]{0,1:T(8,128)(2,1)}) %all-gather.23.cloned.1.call-update) | async-done | bytes 10485776 | tf_op jit(solution)/shard_map/all_gather | solution.py:167
  1032.3 11.9 convolution_convert_fusion
  1044.3 51.2 %reduce-scatter.2.cloned.1.call-done = bf16[448,1280]{1,0:T(8,128)(2,1)} async-done(((bf16[448,5120]{1,0:T(8,128)(2,1)}), bf16[448,1280]{1,0:T(8,128)(2,1)}) %reduce-scatter.2.cloned.1.call-update) | async-done | bytes 1146896 | tf_op jit(solution)/shard_map/reduce_scatter | solution.py:170
  1095.5 1.5 add_convert_fusion
  1097.0 1.9 collective-permute-start
  1098.9 30.3 %collective-permute-done = bf16[448,1280]{1,0:T(8,128)(2,1)S(1)} collective-permute-done((bf16[448,1280]{1,0:T(8,128)(2,1)S(1)}, bf16[448,1280]{1,0:T(8,128)(2,1)S(1)}, u32[]{:S(2)}, u32[]{:S(2)}) %collective-permute-start) | collective-permute-done | bytes 1146912 | tf_op jit(solution)/shard_map/ppermute | solution.py:16
  1129.2 0.2 broadcast_select_fusion
  1129.4 31.0 %collective-permute-done.1 = bf16[448,1280]{1,0:T(8,128)(2,1)S(1)} collective-permute-done((bf16[448,1280]{1,0:T(8,128)(2,1)S(1)}, bf16[448,1280]{1,0:T(8,128)(2,1)S(1)}, u32[]{:S(2)}, u32[]{:S(2)}) %collective-permute-start.1) | collective-permute-done | bytes 1146912 | tf_op jit(solution)/shard_map/ppermute | solution.py:16
  1160.4 0.2 broadcast_select_fusion.1
  1160.7 27.6 %collective-permute-done.2 = bf16[448,1280]{1,0:T(8,128)(2,1)S(1)} collective-permute-done((bf16[448,1280]{1,0:T(8,128)(2,1)S(1)}, bf16[448,1280]{1,0:T(8,128)(2,1)S(1)}, u32[]{:S(2)}, u32[]{:S(2)}) %collective-permute-start.2) | collective-permute-done | bytes 1146912 | tf_op jit(solution)/shard_map/ppermute | solution.py:16
  1188.3 0.2 broadcast_select_fusion.2
  1188.6 27.1 %collective-permute-done.3 = bf16[448,1280]{1,0:T(8,128)(2,1)S(1)} collective-permute-done((bf16[448,1280]{1,0:T(8,128)(2,1)S(1)}, bf16[448,1280]{1,0:T(8,128)(2,1)S(1)}, u32[]{:S(2)}, u32[]{:S(2)}) %collective-permute-start.3) | collective-permute-done | bytes 1146912 | tf_op jit(solution)/shard_map/ppermute | solution.py:16
  1215.6 0.2 broadcast_select_fusion.3
  1215.8 0.5 collective-permute-start.4
  1216.3 23.8 %collective-permute-done.4 = bf16[448,1280]{1,0:T(8,128)(2,1)S(1)} collective-permute-done((bf16[448,1280]{1,0:T(8,128)(2,1)S(1)}, bf16[448,1280]{1,0:T(8,128)(2,1)S(1)}, u32[]{:S(2)}, u32[]{:S(2)}) %collective-permute-start.4) | collective-permute-done | bytes 1146912 | tf_op jit(solution)/shard_map/ppermute | solution.py:16
  1240.1 1.2 broadcast_select_fusion.4
  (65 shorter events, 1.2 us)
Async XLA Ops:
  6.5 26.4 %copy-start.7 = (f32[5120]{0:T(1024)S(1)}, f32[5120]{0:T(1024)}, u32[]{:S(2)}) copy-start(f32[5120]{0:T(1024)} %param.15) | copy-start | bytes 61444
  6.5 24.7 %all-gather.11.cloned.1.call-start = ((), (), s32[]{:S(2)}) async-start(), calls=%async_computation.6 | async-start | bytes 1638400 | tf_op jit(solution)/shard_map/all_gather | solution.py:96
  7.3 65.8 %all-gather.9.cloned.1.call-start = ((), (), s32[]{:S(2)}) async-start(), calls=%async_computation.5 | async-start | bytes 5734400 | tf_op jit(solution)/shard_map/all_gather | solution.py:95
  8.0 220.5 %all-gather.17.cloned.1.call-start = ((), (), s32[]{:S(2)}) async-start(), calls=%async_computation.9 | async-start | bytes 1351680 | tf_op jit(solution)/shard_map/all_gather | solution.py:108
  17.2 9.3 all-to-all-start
  23.9 358.3 %all-gather.13.cloned.1.call-start = ((), (), s32[]{:S(2)}) async-start(), calls=%async_computation.7 | async-start | bytes 1351680 | tf_op jit(solution)/shard_map/all_gather | solution.py:109
  26.5 0.6 copy-start.5
  27.1 508.1 %all-gather.19.cloned.1.call-start = ((), (), s32[]{:S(2)}) async-start(), calls=%async_computation.10 | async-start | bytes 1081344 | tf_op jit(solution)/shard_map/all_gather | solution.py:138
  31.2 1.8 copy-start.1
  73.1 3.7 copy-start
  80.5 152.6 %copy-start.9 = (f32[128]{0:T(128)S(1)}, f32[128]{0:T(128)}, u32[]{:S(2)}) copy-start(f32[128]{0:T(128)} %param.21) | copy-start | bytes 1540
  234.2 153.2 %copy-start.3 = (f32[40,4096]{1,0:T(8,128)S(1)}, f32[40,4096]{1,0:T(8,128)}, u32[]{:S(2)}) copy-start(f32[40,4096]{1,0:T(8,128)} %param.16) | copy-start | bytes 1966084
  234.2 453.8 %all-gather.15.cloned.1.call-start = ((), (), s32[]{:S(2)}) async-start(), calls=%async_computation.8 | async-start | bytes 1081344 | tf_op jit(solution)/shard_map/all_gather | solution.py:139
  386.7 10.8 copy-start.4
  387.3 473.2 %all-gather.21.cloned.1.call-start = ((), (), s32[]{:S(2)}) async-start(), calls=%async_computation.11 | async-start | bytes 10813440 | tf_op jit(solution)/shard_map/all_gather | solution.py:107
  387.4 21.5 %copy-start.10 = (s32[4]{0:T(128)S(1)}, s32[4]{0:T(128)}, u32[]{:S(2)}) copy-start(s32[4]{0:T(128)} %param.22) | copy-start | bytes 52
  387.4 21.8 %copy-start.11 = (s32[4]{0:T(128)S(1)}, s32[4]{0:T(128)}, u32[]{:S(2)}) copy-start(s32[4]{0:T(128)} %param.24) | copy-start | bytes 52
  387.5 21.8 %copy-start.12 = (s32[4]{0:T(128)S(1)}, s32[4]{0:T(128)}, u32[]{:S(2)}) copy-start(s32[4]{0:T(128)} %param.25) | copy-start | bytes 52
  397.4 634.9 %all-gather.23.cloned.1.call-start = ((), (), s32[]{:S(2)}) async-start(), calls=%async_computation.12 | async-start | bytes 10813440 | tf_op jit(solution)/shard_map/all_gather | solution.py:167
  408.9 126.3 %copy-start.8 = (s32[4]{0:T(128)S(1)}, s32[4]{0:T(128)}, u32[]{:S(2)}) copy-start(s32[4]{0:T(128)} %param.23) | copy-start | bytes 52
  408.9 686.6 %reduce-scatter.2.cloned.1.call-start = ((), (), s32[]{:S(2)}) async-start(), calls=%async_computation.13 | async-start | bytes 5734400 | tf_op jit(solution)/shard_map/reduce_scatter | solution.py:170
  869.9 0.7 copy-start.13
  871.8 4.3 copy-start.6
  1044.2 51.2 %copy-start.2 = (bf16[448,1280]{1,0:T(8,128)(2,1)S(1)}, bf16[448,1280]{1,0:T(8,128)(2,1)}, u32[]{:S(2)}) copy-start(bf16[448,1280]{1,0:T(8,128)(2,1)} %param.13) | copy-start | bytes 3440644
  1097.0 32.2 %collective-permute-start = (bf16[448,1280]{1,0:T(8,128)(2,1)S(1)}, bf16[448,1280]{1,0:T(8,128)(2,1)S(1)}, u32[]{:S(2)}, u32[]{:S(2)}) collective-permute-start(bf16[448,1280]{1,0:T(8,128)(2,1)S(1)} %add_convert_fusion), channel_id=1, source_target_pairs={{124,0},{0,4},{4,8},{8,12},{12,16},{16,20},{20,24},{24,28},{28,32}... | collective-permute-start | bytes 3440648 | tf_op jit(solution)/shard_map/ppermute | solution.py:16
  1129.4 31.0 %collective-permute-start.1 = (bf16[448,1280]{1,0:T(8,128)(2,1)S(1)}, bf16[448,1280]{1,0:T(8,128)(2,1)S(1)}, u32[]{:S(2)}, u32[]{:S(2)}) collective-permute-start(bf16[448,1280]{1,0:T(8,128)(2,1)S(1)} %broadcast_select_fusion), channel_id=1, source_target_pairs={{120,0},{124,4},{0,8},{4,12},{8,16},{12,20},{16,24},{20,28},{24,32... | collective-permute-start | bytes 3440648 | tf_op jit(solution)/shard_map/ppermute | solution.py:16
  1160.6 27.7 %collective-permute-start.2 = (bf16[448,1280]{1,0:T(8,128)(2,1)S(1)}, bf16[448,1280]{1,0:T(8,128)(2,1)S(1)}, u32[]{:S(2)}, u32[]{:S(2)}) collective-permute-start(bf16[448,1280]{1,0:T(8,128)(2,1)S(1)} %broadcast_select_fusion.1), channel_id=1, source_target_pairs={{112,0},{116,4},{120,8},{124,12},{0,16},{4,20},{8,24},{12,28},{16,... | collective-permute-start | bytes 3440648 | tf_op jit(solution)/shard_map/ppermute | solution.py:16
  1188.5 27.2 %collective-permute-start.3 = (bf16[448,1280]{1,0:T(8,128)(2,1)S(1)}, bf16[448,1280]{1,0:T(8,128)(2,1)S(1)}, u32[]{:S(2)}, u32[]{:S(2)}) collective-permute-start(bf16[448,1280]{1,0:T(8,128)(2,1)S(1)} %broadcast_select_fusion.2), channel_id=1, source_target_pairs={{96,0},{100,4},{104,8},{108,12},{112,16},{116,20},{120,24},{124,28... | collective-permute-start | bytes 3440648 | tf_op jit(solution)/shard_map/ppermute | solution.py:16
  1215.8 24.3 %collective-permute-start.4 = (bf16[448,1280]{1,0:T(8,128)(2,1)S(1)}, bf16[448,1280]{1,0:T(8,128)(2,1)S(1)}, u32[]{:S(2)}, u32[]{:S(2)}) collective-permute-start(bf16[448,1280]{1,0:T(8,128)(2,1)S(1)} %broadcast_select_fusion.3), channel_id=1, source_target_pairs={{64,0},{68,4},{72,8},{76,12},{80,16},{84,20},{88,24},{92,28},{96,3... | collective-permute-start | bytes 3440648 | tf_op jit(solution)/shard_map/ppermute | solution.py:16
Sparse Core Ops, SparseCore 0:
  9.0 22.1 all-gather.10
  32.9 40.1 all-gather.8
  74.7 153.7 all-gather.16
  230.1 152.1 all-gather.12
  383.8 151.3 all-gather.18
  536.7 151.2 all-gather.14
  689.6 170.8 all-gather.20
  862.1 170.1 all-gather.22
  1044.4 51.0 reduce-scatter.1
where the time goes:
time: 1250 us
  waiting for transfers between devices  1130 us (90%)
  matrix products  41.7 us (3%)
  blocking collectives  27.9 us (2%)
  other arithmetic  21.5 us (2%)
  between operations  13.6 us (1%)
    all_gather x1, waiting for transfers between devices, shards(): lax.all_gather(query_cols, 'rep', axis=0, tiled=True)  171 us
    all_gather x1, waiting for transfers between devices, shards(): lax.all_gather(out_rows, 'rep', axis=1, tiled=True)  152 us
    all_gather x1, waiting for transfers between devices, shards(): lax.all_gather(prompt_values, 'rep', axis=0, tiled=True)  151 us
    all_gather x1, waiting for transfers between devices, shards(): lax.all_gather(key_cols, 'rep', axis=0, tiled=True)  148 us
    all_gather x1, waiting for transfers between devices, shards(): lax.all_gather(value_cols, 'rep', axis=0, tiled=True)  148 us
    ppermute x5, waiting for transfers between devices, from_behind(): return lax.ppermute(block, axis, route)  140 us
    all_gather x1, waiting for transfers between devices, shards(): lax.all_gather(prompt_keys.reshape(prompt_len, -1), 'rep', axis=0, tiled=...  122 us
    reduce_scatter x1, waiting for transfers between devices, shards(): lax.psum_scatter(partial_sum.astype(jnp.bfloat16), 'tp', scatter_dimensio...  51.2 us
  transfers between devices with their start and end apart: 15, of which 15 were waited for; matrix products, arithmetic and copies ran while one was open for 4% of the time, Pallas kernels for 0%

commit v1 on v0

v1 whole, which is shorter than its diff:
```python
import functools

import jax
import jax.numpy as jnp
from jax import lax
from jax.experimental import pallas as pl
from jax.experimental.pallas import tpu as pltpu
from jax.sharding import PartitionSpec as P

PBLK = 64
MESH = pl.DeviceIdType.MESH
ANY = pl.BlockSpec(memory_space=pl.ANY)
VMEM = pl.BlockSpec(memory_space=pltpu.VMEM)
OFFSETS = (0, -1, 1, 2)
META = 16

epsilon = 1e-06
rope_base = 1000000.0


def place():
    rep, tp = lax.axis_index("rep"), lax.axis_index("tp")
    return lax.rem(rep // 4, 4), (tp // 2) * 2 + rep // 16, lax.rem(rep, 4), lax.rem(tp, 2)


def device_at(x, y, z, core):
    return (lax.rem(y, 2) * 16 + x * 4 + z, (y // 2) * 2 + core)


def step(value, by):
    return lax.rem(value + (by + 4), 4)


def greet(peers):
    barrier = pltpu.get_barrier_semaphore()
    for peer in peers:
        pl.semaphore_signal(barrier, inc=1, device_id=peer, device_id_type=MESH)
    pl.semaphore_wait(barrier, len(peers))


def send(source, target, send_sem, recv_sem, device):
    return pltpu.make_async_remote_copy(
        src_ref=source,
        dst_ref=target,
        send_sem=send_sem,
        recv_sem=recv_sem,
        device_id=device,
        device_id_type=MESH,
    )


class Plane:
    COPIES = 72

    def __init__(self, view, send_sems, recv_sems):
        self.view, self.ss, self.rs = view, send_sems, recv_sems
        self.x, self.y, self.z, self.core = place()
        self.started = []

    def block(self, half, first, second, part=None):
        a, b = (first, second) if half == 0 else (second, first)
        return self.view(half, step(self.x, a) * 4 + step(self.z, b), part)

    def toward(self, half, phase, sign):
        if (phase == 0) == (half == 0):
            return device_at(step(self.x, sign), self.y, self.z, self.core)
        return device_at(self.x, self.y, step(self.z, sign), self.core)

    def copy(self, half, number, ref, device):
        at = half * 36 + number
        return send(ref, ref, self.ss.at[at], self.rs.at[at], device)

    def start(self, *args):
        made = self.copy(*args)
        made.start()
        self.started.append(made)

    def sibling(self):
        return device_at(self.x, self.y, self.z, 1 - self.core)

    def share(self, half, o1, o2):
        ref = self.block(half, OFFSETS[o1], OFFSETS[o2])
        self.start(half, 20 + 4 * o1 + o2, ref, self.sibling())

    def spread(self, half, o1):
        ref = self.block(half, OFFSETS[o1], 0)
        self.start(half, 4 + 4 * o1, ref, self.toward(half, 1, 1))
        self.start(half, 5 + 4 * o1, ref, self.toward(half, 1, -1))
        self.share(half, o1, 0)

    def begin(self):
        for half in range(2):
            ref = self.block(half, 0, 0)
            self.start(half, 0, ref, self.toward(half, 0, 1))
            self.start(half, 1, ref, self.toward(half, 0, -1))
        for half in range(2):
            self.spread(half, 0)

    def arrived(self, half, number, ref):
        self.copy(half, number, ref, self.sibling()).wait_recv()

    def first(self):
        for half in range(2):
            self.arrived(half, 0, self.block(half, -1, 0))
            self.start(half, 2, self.block(half, -1, 0, 0), self.toward(half, 0, 1))
            self.arrived(half, 1, self.block(half, 1, 0))
            self.start(half, 3, self.block(half, 1, 0, 1), self.toward(half, 0, -1))
        for half in range(2):
            self.spread(half, 1)
            self.spread(half, 2)

    def opposite(self):
        for half in range(2):
            self.arrived(half, 2, self.block(half, 2, 0, 0))
            self.arrived(half, 3, self.block(half, 2, 0, 1))
            self.spread(half, 3)

    def second(self, o1):
        off, base = OFFSETS[o1], 4 + 4 * o1
        for half in range(2):
            self.arrived(half, base, self.block(half, off, -1))
            self.start(half, base + 2, self.block(half, off, -1, 0), self.toward(half, 1, 1))
            self.arrived(half, base + 1, self.block(half, off, 1))
            self.start(half, base + 3, self.block(half, off, 1, 1), self.toward(half, 1, -1))
            self.share(half, o1, 1)
            self.share(half, o1, 2)

    def second_opposite(self, o1):
        off, base = OFFSETS[o1], 4 + 4 * o1
        for half in range(2):
            self.arrived(half, base + 2, self.block(half, off, 2, 0))
            self.arrived(half, base + 3, self.block(half, off, 2, 1))
            self.share(half, o1, 3)

    def second_all(self):
        self.second(0)
        for o1 in range(1, 4):
            self.second(o1)
            self.second_opposite(o1 - 1)
        self.second_opposite(3)

    def finish(self, shared_block):
        for half in range(2):
            for o1 in range(4):
                for o2 in range(4):
                    a, b = (o1, o2) if half == 0 else (o2, o1)
                    where = step(self.x, OFFSETS[a]) * 4 + step(self.z, OFFSETS[b])
                    self.arrived(half, 20 + 4 * o1 + o2, shared_block(half, where))
        for made in self.started:
            made.wait_send()


def gather_kernel(
    x_ref, win_ref, wout_ref, rows_ref, gin_ref, gout_ref,
    a_send, a_recv, in_send, in_recv, out_send, out_recv, t_send, t_recv, local_sem,
):
    x, y, z, core = place()
    rep, tp = lax.axis_index("rep"), lax.axis_index("tp")
    y_lo, y_hi, plane_at = lax.rem(y, 2), y // 2, x * 4 + z
    sibling = device_at(x, y, z, 1 - core)
    column = [(dy, dc) for dy in range(4) for dc in range(2) if (dy, dc) != (0, 0)]

    def other(dy, dc):
        return step(y, dy), (core if dc == 0 else 1 - core)

    peers = [device_at(x, other(dy, dc)[0], z, other(dy, dc)[1]) for dy, dc in column]
    peers += [device_at(step(x, s), y, z, core) for s in (1, -1)]
    peers += [device_at(x, y, step(z, s), core) for s in (1, -1)]
    greet(peers)

    columns = []
    locals_ = []
    for which, (source, target) in enumerate(((win_ref, gin_ref), (wout_ref, gout_ref))):
        made = pltpu.make_async_copy(
            source.at[y * 2 + core], target.at[core, y_lo, plane_at, tp], local_sem.at[which]
        )
        made.start()
        locals_.append(made)
        sent = []
        for n, (dy, dc) in enumerate(column):
            to_y, to_core = other(dy, dc)
            made = send(
                source.at[to_y * 2 + to_core],
                target.at[to_core, y_lo, plane_at, tp],
                a_send.at[which * 7 + n],
                a_recv.at[which * 7 + n],
                device_at(x, to_y, z, to_core),
            )
            made.start()
            sent.append(made)
        columns.append(sent)

    count, width = x_ref.shape
    cut = count // 32 * 16

    def quarter(at):
        return pl.ds(pl.multiple_of(at * width, 128), width)

    def token_copy(number, source, target, device):
        return send(source, target, t_send.at[number], t_recv.at[number], device)

    home = core == y_lo
    mine = rows_ref.at[:, quarter(tp)]
    up = send(x_ref, mine, t_send.at[0], t_recv.at[core], device_at(x, step(y, 1), z, y_lo))
    down = send(x_ref, mine, t_send.at[1], t_recv.at[2 + core], device_at(x, step(y, -1), z, y_lo))
    up.start()
    down.start()

    @pl.when(home)
    def _():
        pltpu.make_async_copy(x_ref, mine, local_sem.at[2]).start()

    @pl.when(jnp.logical_not(home))
    def _():
        token_copy(4, x_ref, mine, sibling).start()

    def ready(which):
        target = (gin_ref, gout_ref)[which]
        locals_[which].wait()
        for n, (dy, dc) in enumerate(column):
            from_y = step(y, -dy)
            from_core = core if dc == 0 else 1 - core
            ref = target.at[core, lax.rem(from_y, 2), plane_at, (from_y // 2) * 2 + from_core]
            send(ref, ref, a_send.at[which * 7 + n], a_recv.at[which * 7 + n], sibling).wait_recv()

    def viewer(target, owner):
        def view(half, where, part=None):
            if part is None:
                return target.at[owner, half, where]
            return target.at[owner, half, where, pl.ds(part * 2, 2)]

        return view

    inward = Plane(viewer(gin_ref, core), in_send, in_recv)
    outward = Plane(viewer(gout_ref, core), out_send, out_recv)
    ready(0)
    inward.begin()
    inward.first()
    inward.opposite()
    ready(1)
    outward.begin()

    def away_blocks():
        below, above = step(y, -1), step(y, 1)
        for k in range(2):
            low = (below // 2) * 2 + k
            high = (above // 2) * 2 + k
            yield k, low, high, below, above

    @pl.when(jnp.logical_not(home))
    def _():
        for k, low, high, below, above in away_blocks():
            ref = rows_ref.at[:, quarter(low)]
            token_copy(k, ref, ref, sibling).wait_recv()
            ref = rows_ref.at[pl.ds(0, cut), quarter(low)]
            token_copy(5 + k, ref, ref, device_at(x, above, z, core)).start()
            ref = rows_ref.at[:, quarter(high)]
            token_copy(2 + k, ref, ref, sibling).wait_recv()
            ref = rows_ref.at[pl.ds(cut, count - cut), quarter(high)]
            token_copy(7 + k, ref, ref, device_at(x, below, z, core)).start()

    inward.second_all()
    outward.first()
    outward.opposite()
    outward.second_all()

    @pl.when(jnp.logical_not(home))
    def _():
        for k, low, high, below, above in away_blocks():
            ref = rows_ref.at[pl.ds(0, cut), quarter(low)]
            token_copy(5 + k, ref, ref, sibling).wait_send()
            ref = rows_ref.at[pl.ds(cut, count - cut), quarter(high)]
            token_copy(7 + k, ref, ref, sibling).wait_send()
        token_copy(4, x_ref, mine, sibling).wait_send()

    @pl.when(home)
    def _():
        opposite = 1 - y_hi
        for k in range(2):
            at = quarter(opposite * 2 + k)
            ref = rows_ref.at[pl.ds(0, cut), at]
            token_copy(5 + k, ref, ref, sibling).wait_recv()
            ref = rows_ref.at[pl.ds(cut, count - cut), at]
            token_copy(7 + k, ref, ref, sibling).wait_recv()
        ref = rows_ref.at[:, quarter(y_hi * 2 + 1 - core)]
        token_copy(4, ref, ref, sibling).wait_recv()
        pltpu.make_async_copy(x_ref, mine, local_sem.at[2]).wait()

    up.wait_send()
    down.wait_send()
    for sent in columns:
        for made in sent:
            made.wait_send()
    inward.finish(viewer(gin_ref, 1 - core))
    outward.finish(viewer(gout_ref, 1 - core))


def gather_all(rows, win, wout):
    count, width = rows.shape
    sems = [14, 14, Plane.COPIES, Plane.COPIES, Plane.COPIES, Plane.COPIES, 9, 9, 3]
    return pl.pallas_call(
        gather_kernel,
        name="gather_all",
        out_shape=(
            jax.ShapeDtypeStruct((count, 4 * width), rows.dtype),
            jax.ShapeDtypeStruct((2, 2, 16, 4) + win.shape[1:], win.dtype),
            jax.ShapeDtypeStruct((2, 2, 16, 4) + wout.shape[1:], wout.dtype),
        ),
        in_specs=[ANY] * 3,
        out_specs=(ANY,) * 3,
        scratch_shapes=[pltpu.SemaphoreType.DMA((n,)) for n in sems],
        compiler_params=pltpu.CompilerParams(collective_id=0, has_side_effects=True),
    )(rows, win, wout)


def prompt_kernel(own_ref, all_ref, send_sems, recv_sems, local_sem):
    x, y, z, core = place()
    peers = [device_at(x, y, z, 1 - core)]
    peers += [device_at(step(x, s), y, z, core) for s in (1, -1)]
    peers += [device_at(x, y, step(z, s), core) for s in (1, -1)]
    greet(peers)
    made = pltpu.make_async_copy(own_ref, all_ref.at[core, x * 4 + z], local_sem.at[0])
    made.start()
    made.wait()

    def viewer(owner):
        def view(half, where, part=None):
            rows = pl.ds(half * 64, 64) if part is None else pl.ds(half * 64 + part * 32, 32)
            return all_ref.at[owner, where, rows]

        return view

    plane = Plane(viewer(core), send_sems, recv_sems)
    plane.begin()
    plane.first()
    plane.opposite()
    plane.second_all()
    plane.finish(viewer(1 - core))


def gather_prompts(own):
    sems = [Plane.COPIES, Plane.COPIES, 1]
    return pl.pallas_call(
        prompt_kernel,
        name="gather_prompts",
        out_shape=jax.ShapeDtypeStruct((2, 16) + own.shape, own.dtype),
        in_specs=[ANY],
        out_specs=ANY,
        scratch_shapes=[pltpu.SemaphoreType.DMA((n,)) for n in sems],
        compiler_params=pltpu.CompilerParams(collective_id=1, has_side_effects=True),
    )(own)


CHUNKS = 4
ORDERS = (
    ("z1", "x2", "y1", "z2", "x1"),
    ("x1", "z2", "x2", "y1", "z1"),
    ("y1", "z1", "x1", "x2", "z2"),
    ("z2", "y1", "z1", "x1", "x2"),
)
SIGNS = (1, -1, 1, -1)


def level_bits(shift, sign):
    odd = shift % 2 == 1
    far = (shift >= 2) if sign == 1 else ((shift == 1) | (shift == 2))
    return odd, far


def move_masks(shift_rows, rep):
    z, x = rep % 4, rep // 4 % 4
    rows = shift_rows.shape[0] // CHUNKS
    masks = []
    for chunk in range(CHUNKS):
        sign = SIGNS[chunk]
        shift = shift_rows[chunk * rows : (chunk + 1) * rows]
        shift_z = shift % 4
        odd_z, far_z = level_bits(shift_z, sign)
        for at, level in enumerate(ORDERS[chunk]):
            later = ORDERS[chunk][at + 1 :]
            end_z = z
            if "z1" in later:
                end_z = end_z + sign * odd_z.astype(jnp.int32)
            if "z2" in later:
                end_z = end_z + 2 * far_z.astype(jnp.int32)
            end_z = (end_z + 4) % 4
            carry_z = (end_z < shift_z).astype(jnp.int32)
            need_x = shift // 4 % 4 + carry_z
            shift_x = need_x % 4
            odd_x, far_x = level_bits(shift_x, sign)
            end_x = x
            if "x1" in later:
                end_x = end_x + sign * odd_x.astype(jnp.int32)
            if "x2" in later:
                end_x = end_x + 2 * far_x.astype(jnp.int32)
            end_x = (end_x + 4) % 4
            carry_x = (end_x < need_x).astype(jnp.int32)
            shift_y = (shift // 16 + carry_x) % 2
            masks.append(
                {"z1": odd_z, "z2": far_z, "x1": odd_x, "x2": far_x, "y1": shift_y == 1}[level]
            )
    masks = jnp.stack(masks).astype(jnp.float32)
    return jnp.broadcast_to(
        masks.reshape(CHUNKS, len(ORDERS[0]), rows, 1), (CHUNKS, len(ORDERS[0]), rows, 128)
    )


def return_kernel(
    part_ref, tokens_ref, mask_ref, out_ref,
    raw, final, summed, held, landed,
    raw_send, raw_recv, fin_send, fin_recv, sib_send, sib_recv, move_send, move_recv,
):
    x, y, z, core = place()
    y_lo, y_hi = lax.rem(y, 2), y // 2
    width = tokens_ref.shape[1]
    rows = tokens_ref.shape[0] // CHUNKS
    above, below = step(y, 1), step(y, -1)
    sibling = device_at(x, y, z, 1 - core)
    peers = [device_at(x, at, z, k) for at in (above, below) for k in range(2)] + [sibling]
    peers += [device_at(step(x, s), y, z, core) for s in (1, -1, 2)]
    peers += [device_at(x, y, step(z, s), core) for s in (1, -1, 2)]
    greet(peers)
    home = core == y_lo

    def block(chunk):
        return pl.ds(chunk * rows, rows)

    def part(chunk, quarter):
        return part_ref.at[block(chunk), pl.ds(pl.multiple_of(quarter * width, 128), width)]

    def raw_copy(chunk, slot):
        quarter = (1 - y_hi) * 2 + slot
        to = device_at(x, (above, below)[slot], z, core)
        at = slot * CHUNKS + chunk
        return send(part(chunk, quarter), raw.at[slot, block(chunk)], raw_send.at[at], raw_recv.at[at], to)

    def sibling_copy(chunk):
        return send(
            part(chunk, y_hi * 2 + 1 - core), final.at[2, block(chunk)],
            sib_send.at[chunk], sib_recv.at[chunk], sibling,
        )

    def final_copy(chunk, slot, k):
        to_y = (above, below)[slot]
        if slot == k:
            source = summed.at[slot, block(chunk)]
        else:
            source = part(chunk, (to_y // 2) * 2 + k)
        at = slot * CHUNKS + chunk
        return send(
            source, final.at[slot, block(chunk)],
            fin_send.at[at + k * 2 * CHUNKS], fin_recv.at[at], device_at(x, to_y, z, k),
        )

    @pl.when(home)
    def _():
        for chunk in range(CHUNKS):
            raw_copy(chunk, 0).start()
            raw_copy(chunk, 1).start()
            sibling_copy(chunk).start()

    @pl.when(jnp.logical_not(home))
    def _():
        for chunk in range(CHUNKS):
            for slot in range(2):
                final_copy(chunk, slot, 1 - slot).start()
        for chunk in range(CHUNKS):
            for slot in range(2):
                raw_copy(chunk, slot).wait_recv()
                quarter = ((above, below)[slot] // 2) * 2 + slot
                summed[slot, block(chunk)] = (
                    part(chunk, quarter)[...].astype(jnp.float32)
                    + raw[slot, block(chunk)].astype(jnp.float32)
                ).astype(jnp.bfloat16)
                final_copy(chunk, slot, slot).start()

    def target(level, sign):
        by = sign if level[1] == "1" else 2
        if level[0] == "z":
            return device_at(x, y, step(z, by), core)
        if level[0] == "x":
            return device_at(step(x, by), y, z, core)
        return device_at(x, y_hi * 2 + 1 - y_lo, z, core)

    def move(chunk, at):
        number = at * CHUNKS + chunk
        return send(
            held.at[at, block(chunk)], landed.at[at, block(chunk)],
            move_send.at[number], move_recv.at[number], target(ORDERS[chunk][at], SIGNS[chunk]),
        )

    steps = len(ORDERS[0])
    for chunk in range(CHUNKS):
        for slot in range(2):
            final_copy(chunk, slot, 0).wait_recv()

        @pl.when(home)
        def _():
            final[2, block(chunk)] = part(chunk, y_hi * 2 + core)[...]

        @pl.when(jnp.logical_not(home))
        def _():
            sibling_copy(chunk).wait_recv()

        total = final[0, block(chunk)].astype(jnp.float32) + final[1, block(chunk)].astype(jnp.float32)
        total = total + final[2, block(chunk)].astype(jnp.float32)
        held[0, block(chunk)] = (
            tokens_ref[block(chunk)].astype(jnp.float32) + total
        ).astype(jnp.bfloat16)
        move(chunk, 0).start()

    for at in range(steps):
        for chunk in range(CHUNKS):
            move(chunk, at).wait_recv()
            taken = mask_ref[chunk, at][:, :1] > 0.5
            chosen = jnp.where(
                taken,
                landed[at, block(chunk)].astype(jnp.float32),
                held[at, block(chunk)].astype(jnp.float32),
            ).astype(jnp.bfloat16)
            if at < steps - 1:
                held[at + 1, block(chunk)] = chosen
                move(chunk, at + 1).start()
            else:
                out_ref[block(chunk)] = chosen

    for at in range(steps):
        for chunk in range(CHUNKS):
            move(chunk, at).wait_send()

    @pl.when(home)
    def _():
        for chunk in range(CHUNKS):
            raw_copy(chunk, 0).wait_send()
            raw_copy(chunk, 1).wait_send()
            sibling_copy(chunk).wait_send()

    @pl.when(jnp.logical_not(home))
    def _():
        for chunk in range(CHUNKS):
            for slot in range(2):
                for k in range(2):
                    final_copy(chunk, slot, k).wait_send()


def return_rows(part, tokens, masks):
    count, width = tokens.shape
    steps = len(ORDERS[0])
    shapes = [2, 3, 2, steps, steps]
    sems = [2, 2, 4, 2, 1, 1, steps, steps]
    return pl.pallas_call(
        return_kernel,
        name="return_rows",
        out_shape=jax.ShapeDtypeStruct(tokens.shape, tokens.dtype),
        in_specs=[VMEM] * 3,
        out_specs=VMEM,
        scratch_shapes=[pltpu.VMEM((n, count, width), jnp.bfloat16) for n in shapes]
        + [pltpu.SemaphoreType.DMA((n * CHUNKS,)) for n in sems],
        compiler_params=pltpu.CompilerParams(
            collective_id=2, has_side_effects=True, vmem_limit_bytes=48 * 2**20
        ),
    )(part, tokens, masks)


def rms_rows(values, gain_row):
    floats = values.astype(jnp.float32)
    scaled = lax.rsqrt(jnp.mean(floats * floats, axis=-1, keepdims=True) + epsilon)
    return floats * scaled * gain_row


def rotary(values, positions):
    half_size = values.shape[-1] // 2
    spread = jnp.arange(half_size, dtype=jnp.float32) * (2.0 / values.shape[-1])
    frequency = rope_base ** (-spread)
    angles = positions.astype(jnp.float32)[:, None] * frequency[None, :]
    cosine = jnp.cos(angles)[:, None, :]
    sine_part = jnp.sin(angles)[:, None, :]
    front_half = values[..., :half_size]
    back_half = values[..., half_size:]
    return jnp.concatenate(
        [front_half * cosine - back_half * sine_part, back_half * cosine + front_half * sine_part],
        axis=-1,
    )


def slot_layout(seq_lengths, row_count):
    ends_at = jnp.cumsum(seq_lengths)
    starts_at = ends_at - seq_lengths
    position = jnp.arange(row_count, dtype=jnp.int32)
    slot_of = jnp.sum((position[:, None] >= ends_at[None, :]).astype(jnp.int32), axis=1)
    onehot = (
        slot_of[:, None] == jnp.arange(seq_lengths.shape[0], dtype=jnp.int32)[None, :]
    ).astype(jnp.int32)
    within = position - jnp.sum(onehot * starts_at[None, :], axis=1)
    return (slot_of, within, onehot)


def attend(
    queries, own_keys, own_values, shared_keys, shared_values, slot_of, prefix_len, prompt_len
):
    row_count = queries.shape[0]
    head_size = queries.shape[-1]
    all_keys = jnp.concatenate([shared_keys, own_keys], axis=0)
    all_values = jnp.concatenate([shared_values, own_values], axis=0)
    shared_index = jnp.arange(shared_keys.shape[0], dtype=jnp.int32)
    shared_mask = ((shared_index // prompt_len)[None, :] == slot_of[:, None]) & (
        (shared_index % prompt_len)[None, :] < prefix_len[:, None]
    )
    position = jnp.arange(row_count, dtype=jnp.int32)
    own_mask = (slot_of[None, :] == slot_of[:, None]) & (position[None, :] <= position[:, None])
    allowed = jnp.concatenate([shared_mask, own_mask], axis=1)
    scores = jnp.einsum(
        "rgd,nd->grn", queries, all_keys, preferred_element_type=jnp.float32
    ) * head_size ** (-0.5)
    weights = jnp.where(allowed[None], jnp.exp(scores), 0.0)
    weighted = (weights / jnp.sum(weights, axis=-1, keepdims=True)).astype(jnp.bfloat16)
    blended = jnp.einsum("grn,nd->rgd", weighted, all_values, preferred_element_type=jnp.float32)
    return blended.reshape(row_count, -1).astype(jnp.bfloat16)


def shards(
    tokens,
    prompt_rows,
    norm_gain,
    w_query,
    w_key,
    w_value,
    w_out,
    q_gain,
    k_gain,
    seq_lengths,
    prompt_group,
    prompt_blocks,
    dest_offset,
):
    row_count, width = tokens.shape
    prompt_len = prompt_rows.shape[0]
    head_size = q_gain.shape[0]
    slot_count = seq_lengths.shape[0]
    depth = w_query.shape[0]
    groups = w_key.shape[1] // head_size
    rep = lax.axis_index("rep")

    halves = w_query.astype(jnp.bfloat16).reshape(depth, groups, 2, -1)
    key_cols = w_key.astype(jnp.bfloat16).reshape(depth, groups, 1, head_size)
    value_cols = w_value.astype(jnp.bfloat16).reshape(depth, groups, 1, head_size)
    win = jnp.concatenate([halves, jnp.concatenate([key_cols, value_cols], axis=2)], axis=3)
    win = win.transpose(1, 2, 0, 3).reshape(2 * groups, depth, -1)
    wout = w_out.astype(jnp.bfloat16).reshape(2 * groups, -1, depth).transpose(0, 2, 1)
    meta = jnp.concatenate([prompt_group, prompt_blocks]).astype(jnp.bfloat16)
    meta = jnp.pad(meta[None, :], ((0, META - 1), (0, width - 2 * slot_count)))
    rows, gin, gout = gather_all(jnp.concatenate([tokens, prompt_rows, meta], axis=0), win, wout)

    meta = rows[row_count + prompt_len, : 2 * slot_count].astype(jnp.int32)
    group_here, blocks_here = meta[:slot_count], meta[slot_count:]
    normed = rms_rows(rows[: row_count + prompt_len], norm_gain).astype(jnp.bfloat16)
    features = normed.shape[1]
    gin = gin.reshape(2, features, -1)
    left = jnp.dot(normed, gin[0], preferred_element_type=jnp.float32)
    right = jnp.dot(normed, gin[1], preferred_element_type=jnp.float32)
    half_width = left.shape[1] - head_size
    query_sum = jnp.concatenate([left[:row_count, :half_width], right[:row_count, :half_width]], axis=1)
    key_sum, values_all = left[:, half_width:], right[:, half_width:].astype(jnp.bfloat16)
    q_heads = query_sum.shape[1] // head_size

    slot_of, within, onehot = slot_layout(seq_lengths, row_count)
    prefix_len = jnp.sum(onehot * (blocks_here * PBLK)[None, :], axis=1)
    positions = prefix_len + within
    queries = rotary(rms_rows(query_sum.reshape(row_count, q_heads, head_size), q_gain), positions)
    queries = queries.astype(jnp.bfloat16)
    all_positions = jnp.concatenate([positions, jnp.arange(prompt_len, dtype=jnp.int32)])
    keys_all = rotary(rms_rows(key_sum[:, None], k_gain), all_positions).astype(jnp.bfloat16)[:, 0]
    shared = gather_prompts(
        jnp.concatenate([keys_all[row_count:], values_all[row_count:]], axis=1)
    ).reshape(-1, prompt_len, 2 * head_size)
    shared = jnp.concatenate(
        [lax.dynamic_index_in_dim(shared, group_here[j], 0, keepdims=False) for j in range(slot_count)],
        axis=0,
    )
    blended = attend(
        queries, keys_all[:row_count], values_all[:row_count],
        shared[:, :head_size], shared[:, head_size:], slot_of, prefix_len, prompt_len,
    )
    gout = gout.reshape(2, features, -1)
    half_rows = gout.shape[2]
    part = lax.dot_general(
        blended[:, :half_rows], gout[0], (((1,), (1,)), ((), ())), preferred_element_type=jnp.float32
    ) + lax.dot_general(
        blended[:, half_rows:], gout[1], (((1,), (1,)), ((), ())), preferred_element_type=jnp.float32
    )
    shift_rows = jnp.sum(onehot * dest_offset[None, :], axis=1)
    return return_rows(part.astype(jnp.bfloat16), tokens, move_masks(shift_rows, rep))


def solution(mesh):
    return jax.shard_map(
        shards,
        mesh=mesh,
        in_specs=(
            P("rep", "tp"),
            P("rep", "tp"),
            P(),
            P(("rep", "tp"), None),
            P(("rep", "tp"), None),
            P(("rep", "tp"), None),
            P(None, ("rep", "tp")),
            P(),
            P(),
            P(),
            P("rep"),
            P("rep"),
            P(),
        ),
        out_specs=P("rep", "tp"),
        check_vma=False,
    )
```

time: 1250 us -> 307 us (0.25)
  waiting for transfers between devices: 1130 us -> 0 us
  Pallas kernels: 0 us -> 204 us
  blocking collectives: 27.9 us -> 0 us
  local copies, waits for them, and re-layouts: 3.36 us -> 27.9 us
    all_gather x8 -> x0, waiting for transfers between devices: 935 us -> none  [the longest x1 171 us: shards(): lax.all_gather(query_cols, 'rep', axis=0, tiled=True)]
    pallas_call x0 -> x3, Pallas kernels: none -> 204 us  [the longest x1 95.9 us: return_rows(): pl.pallas_call(return_kernel, name='return_rows', out_shape=jax.ShapeDtyp...]
    ppermute x5 -> x0, waiting for transfers between devices: 140 us -> none  [from_behind(): return lax.ppermute(block, axis, route)]
    reduce_scatter x1 -> x0, waiting for transfers between devices: 51.2 us -> none  [shards(): lax.psum_scatter(partial_sum.astype(jnp.bfloat16), 'tp', scatter_dimensio...]
    all_to_all x3 -> x0, blocking collectives: 27.9 us -> none  [the longest x1 11.3 us: shards(): lax.all_to_all(w_out.astype(jnp.bfloat16), 'tp', split_axis=0, concat_axi...]
    slice x1 -> x8, local copies, waits for them, and re-layouts: 0.6 us -> 23.5 us  [the longest x1 9.83 us: shards(): left = jnp.dot(normed, gin[0], preferred_element_type=jnp.float32)]
    dot_general x8 -> x6, matrix products: 41.7 us -> 34.3 us  [the longest x1 8.99 us: shards(): left = jnp.dot(normed, gin[0], preferred_element_type=jnp.float32)]
  transfers between devices with their start and end apart: 15 -> 0, of which waited for: 15 -> 0; matrix products, arithmetic and copies ran while one was open for 4% -> 0% of each run, Pallas kernels for 0% -> 0%
where the time goes in v1:
time: 307 us; the launch traced here: 301 us
  Pallas kernels  204 us (66%)
  matrix products  34.3 us (11%)
  local copies, waits for them, and re-layouts  27.9 us (9%)
  other arithmetic  27.5 us (9%)
  between operations  7.85 us (3%)
    pallas_call x1, Pallas kernels, return_rows(): pl.pallas_call(return_kernel, name='return_rows', out_shape=jax.ShapeDtyp...  95.9 us
    pallas_call x1, Pallas kernels, gather_all(): pl.pallas_call(gather_kernel, name='gather_all', out_shape=(jax.ShapeDtyp...  83.2 us
    pallas_call x1, Pallas kernels, gather_prompts(): pl.pallas_call(prompt_kernel, name='gather_prompts', out_shape=jax.ShapeD...  24.8 us
    slice x1, local copies, waits for them, and re-layouts, shards(): left = jnp.dot(normed, gin[0], preferred_element_type=jnp.float32)  9.83 us
    slice x1, local copies, waits for them, and re-layouts, shards(): gout[1]  9.39 us
    dot_general x1, matrix products, shards(): left = jnp.dot(normed, gin[0], preferred_element_type=jnp.float32)  8.99 us
    dot_general x1, matrix products, shards(): lax.dot_general(blended[:, half_rows:], gout[1], (((1,), (1,)), ((), ()))...  7.34 us

profile of v1, /device:TPU:16, one launch (start us, length us, event | category | flops | bytes accessed | tf_op | source)
XLA Modules:
  0.0 301.5 jit_solution(13590889563746753753)
XLA Ops:
  0.0 0.9 reduce-window.8
  1.0 0.7 bitcast_subtract_fusion
  1.6 0.7 convert_bitcast_fusion
  2.3 0.1 convert_reduce_fusion
  2.4 0.1 fusion.40
  2.5 0.9 convert_element_type.149
  3.4 0.9 convert_element_type.150
  4.3 0.2 fusion.18
  4.5 1.1 convert_element_type.148
  5.6 0.2 reshape.361
  5.9 0.1 copy.40
  6.0 0.8 maximum_maximum_fusion
  6.8 1.1 convert_element_type.151
  7.9 0.8 copy.54
  8.6 1.3 pad_maximum_fusion.1.x_ref
  9.9 83.2 %gather_all.1 = (bf16[592,5120]{1,0:T(8,128)(2,1)}, bf16[2,2,16,4,40,640]{5,4,3,2,1,0:T(8,128)(2,1)}, bf16[2,2,16,4,40,512]{5,4,3,2,1,0:T(8,128)(2,1)}) custom-call(bf16[592,1280]{1,0:T(8,128)(2,1)} %pad_maximum_fusion.1.x_ref, bf16[8,40,640]{2,1,0:T(8,128)(2,1)} %bitcast.134, bf16[8,40,512]{2,1,0:T(8,128)(2,1)} %bitcast.135), custom_call_target="tpu_custom_call" | custom-call | tf_op jit(solution)/shard_map/gather_all/pallas_call | solution.py:301
  93.2 9.8 %fusion.118 = (bf16[1,2,16,4,40,640]{5,4,3,2,1,0:T(8,128)(2,1)}, bf16[1,2,16,4,40,640]{5,4,3,2,1,0:T(8,128)(2,1)}) fusion(bf16[2,2,16,4,40,640]{5,4,3,2,1,0:T(8,128)(2,1)} %get-tuple-element.9), kind=kLoop, calls=%fused_computation.357 | loop fusion | bytes 26214400 | tf_op jit(solution)/shard_map/slice | solution.py:659
  103.0 0.7 slice_convert_fusion
  103.7 0.1 multiply_bitcast_fusion.1
  103.8 0.6 fusion.121
  111.8 4.1 %fusion.1 = f32[576]{0:T(1024)S(1)} fusion(bf16[592,5120]{1,0:T(8,128)(2,1)} %get-tuple-element.8), kind=kLoop, calls=%fused_computation.5 | loop fusion | flops 8846784 | bytes 5900544 | tf_op jit(solution)/shard_map/reduce_sum | solution.py:567
  115.9 9.0 %fusion.12 = f32[576,640]{1,0:T(8,128)S(1)} fusion(bf16[5120,640]{1,0:T(8,128)(2,1)} %bitcast.127, f32[5120]{0:T(1024)S(1)} %copy-done.10, f32[576]{0:T(1024)S(1)} %add_rsqrt_fusion.2, bf16[592,5120]{1,0:T(8,128)(2,1)} %get-tuple-element.8), kind=kOutput, calls=%fused_computation.23 | convolution fusion | flops 3786670080 | bytes 13949184 | tf_op jit(solution)/shard_map/dot_general | solution.py:659
  124.9 0.0 copy-start.7
  124.9 0.0 copy-start.8
  125.0 5.7 %fusion.122 = (bf16[576,640]{1,0:T(8,128)(2,1)}, f32[576,640]{1,0:T(8,128)S(1)}) fusion(bf16[5120,640]{1,0:T(8,128)(2,1)S(1)} %bitcast.126, f32[5120]{0:T(1024)S(1)} %copy-done.10, f32[576]{0:T(1024)S(1)} %add_rsqrt_fusion.2, bf16[592,5120]{1,0:T(8,128)(2,1)S(1)} %bitcast.129), kind=kOutput, calls=%fused_computation.361 | convolution fusion | flops 3787038720 | bytes 14688256 | tf_op jit(solution)/shard_map/dot_general | solution.py:660
  130.6 0.1 slice.154
  130.8 0.2 multiply_reduce_fusion.1
  131.0 0.1 select_reduce_fusion
  131.1 0.1 negate_select_fusion.3
  131.2 0.1 or_bitcast_fusion
  131.4 0.1 compare_bitcast_fusion.12
  131.4 0.1 compare_bitcast_fusion.2
  131.5 0.1 compare_bitcast_fusion.5
  131.7 0.1 stack.83
  131.8 0.1 add_convert_fusion.2
  131.9 0.8 slice.149
  132.7 1.5 slice.151
  134.2 0.2 compare_and_fusion
  134.5 0.9 pad_add_fusion
  135.3 1.1 multiply_bitcast_fusion
  136.4 1.2 slice.153
  137.7 1.6 fusion.27
  139.3 0.1 maximum_bitcast_fusion.4
  139.4 0.7 fusion.34
  140.1 0.6 pad_maximum_fusion.4.own_ref
  140.8 1.6 multiply_cosine_fusion.1
  142.3 0.3 broadcast_in_dim.12.mask_ref
  142.7 0.0 copy-start.9
  142.7 1.5 fusion.7
  144.2 0.4 copy.49
  144.6 0.5 multiply_reduce_fusion
  145.2 0.1 copy.43
  145.3 2.0 fusion.5
  147.3 2.0 subtract_convert_fusion
  149.3 24.8 %gather_prompts.1 = bf16[2,16,128,256]{3,2,1,0:T(8,128)(2,1)} custom-call(bf16[128,256]{1,0:T(8,128)(2,1)} %pad_maximum_fusion.4.own_ref), custom_call_target="tpu_custom_call" | custom-call | tf_op jit(solution)/shard_map/gather_prompts/pallas_call | solution.py:343
  174.1 1.0 dynamic-slice_bitcast_fusion.3
  175.1 9.4 %fusion.119 = (bf16[1,2,16,4,40,512]{5,4,3,2,1,0:T(8,128)(2,1)}, bf16[1,2,16,4,40,512]{5,4,3,2,1,0:T(8,128)(2,1)}) fusion(bf16[2,2,16,4,40,512]{5,4,3,2,1,0:T(8,128)(2,1)} %get-tuple-element.10), kind=kLoop, calls=%fused_computation.358 | loop fusion | bytes 20971520 | tf_op jit(solution)/shard_map/slice | solution.py:689
  184.5 5.7 %fusion = (f32[8,448]{1,0:T(8,128)S(1)}, f32[960,448,8]{0,1,2:T(8,128)S(1)}) fusion(pred[448,960]{1,0:T(8,128)(4,1)} %pad_add_fusion, bf16[448,8,64]{2,0,1:T(8,128)(2,1)} %get-tuple-element.43, bf16[448,8,64]{2,0,1:T(8,128)(2,1)S(1)} %copy-done.3, bf16[448,128]{1,0:T(8,128)(2,1)} %fusion.34, bf16[512,128]{1,0:T(8,128)(2,1)S(1)} %get-tuple-element.53), kind=kOutput, calls=%fused_computation.4 | convolution fusion | flops 893448704 | bytes 15370240 | tf_op jit(solution)/shard_map/rgd,nd->grn/dot_general | solution.py:612
  190.2 4.1 %fusion.9 = bf16[8,56,8,128]{3,2,1,0:T(8,128)(2,1)S(1)} fusion(f32[960,448,8]{0,1,2:T(8,128)S(1)} %get-tuple-element.79, f32[8,448]{1,0:T(8,128)S(1)} %get-tuple-element.78, pred[448,960]{1,0:T(8,128)(4,1)S(1)} %copy-done.4, bf16[448,128]{1,0:T(8,128)(2,1)S(1)} %copy-done.6, bf16[512,128]{1,0:T(8,128)(2,1)S(1)} %get-tuple-element.52), kind=kOutput, calls=%fused_computation.21 | convolution fusion | flops 895516672 | bytes 15370240 | tf_op jit(solution)/shard_map/grn,nd->rgd/dot_general | solution.py:617
  194.3 0.2 copy.53
  194.6 2.6 fusion.20
  197.2 7.3 %add_convert_fusion.part_ref = bf16[448,5120]{1,0:T(8,128)(2,1)} fusion(f32[448,5120]{1,0:T(8,128)S(1)} %fusion.20, bf16[5120,512]{1,0:T(8,128)(2,1)} %bitcast.130, bf16[448,1024]{1,0:T(8,128)(2,1)S(1)} %bitcast.133), kind=kOutput, calls=%fused_computation.8 | convolution fusion | flops 2353397760 | bytes 19464192 | tf_op jit(solution)/shard_map/dot_general | solution.py:688
  204.5 95.9 %return_rows.1 = bf16[448,1280]{1,0:T(8,128)(2,1)S(1)} custom-call(bf16[448,5120]{1,0:T(8,128)(2,1)} %add_convert_fusion.part_ref, bf16[448,1280]{1,0:T(8,128)(2,1)S(1)} %copy-done, f32[4,5,112,128]{3,2,1,0:T(8,128)S(1)} %broadcast_in_dim.12.mask_ref), custom_call_target="tpu_custom_call" | custom-call | tf_op jit(solution)/shard_map/return_rows/pallas_call | solution.py:551
  300.4 1.0 copy.56
  (57 shorter events, 0.4 us)
Async XLA Ops:
  0.0 8.6 %copy-start = (bf16[448,1280]{1,0:T(8,128)(2,1)S(1)}, bf16[448,1280]{1,0:T(8,128)(2,1)}, u32[]{:S(2)}) copy-start(bf16[448,1280]{1,0:T(8,128)(2,1)} %tokens_ref.1) | copy-start | bytes 3440644
  0.0 8.6 %copy-start.5 = (bf16[128,1280]{1,0:T(8,128)(2,1)S(1)}, bf16[128,1280]{1,0:T(8,128)(2,1)}, u32[]{:S(2)}) copy-start(bf16[128,1280]{1,0:T(8,128)(2,1)} %param.14) | copy-start | bytes 983044
  103.0 12.9 %copy-start.10 = (f32[5120]{0:T(1024)S(1)}, f32[5120]{0:T(1024)}, u32[]{:S(2)}) copy-start(f32[5120]{0:T(1024)} %param.15) | copy-start | bytes 61444
  111.8 13.1 %slice-start.2 = ((s8[6553600]{0:T(1024)(128)(4,1)}), s8[2359296]{0:T(1024)(128)(4,1)S(1)}, s32[]{:S(2)}) async-start(s8[6553600]{0:T(1024)(128)(4,1)} %bitcast.124), calls=%async_computation.2 | async-start | bytes 4718592
  111.8 13.1 %slice-start.4 = ((s8[6062080]{0:T(1024)(128)(4,1)}), s8[4194304]{0:T(1024)(128)(4,1)S(1)}, s32[]{:S(2)}) async-start(s8[6062080]{0:T(1024)(128)(4,1)} %bitcast.128), calls=%async_computation.4 | async-start | bytes 8388608
  115.9 9.0 %slice-start.3 = ((s8[6553600]{0:T(1024)(128)(4,1)}), s8[4194304]{0:T(1024)(128)(4,1)S(1)}, s32[]{:S(2)}) async-start(s8[6553600]{0:T(1024)(128)(4,1)} %bitcast.124), calls=%async_computation.3 | async-start | bytes 8388608
  115.9 9.0 %slice-start.5 = ((s8[6062080]{0:T(1024)(128)(4,1)}), s8[1867776]{0:T(1024)(128)(4,1)S(1)}, s32[]{:S(2)}) async-start(s8[6062080]{0:T(1024)(128)(4,1)} %bitcast.128), calls=%async_computation.5 | async-start | bytes 3735552
  124.9 5.8 %copy-start.1 = (f32[576,640]{1,0:T(8,128)}, f32[576,640]{1,0:T(8,128)S(1)}, u32[]{:S(2)}) copy-start(f32[576,640]{1,0:T(8,128)S(1)} %fusion.12) | copy-start | bytes 4423684
  124.9 6.0 %copy-start.7 = (s32[4]{0:T(128)S(1)}, s32[4]{0:T(128)}, u32[]{:S(2)}) copy-start(s32[4]{0:T(128)} %param.25) | copy-start | bytes 52
  124.9 10.4 %copy-start.8 = (f32[128]{0:T(128)S(1)}, f32[128]{0:T(128)}, u32[]{:S(2)}) copy-start(f32[128]{0:T(128)} %param.21) | copy-start | bytes 1540
  142.7 2.6 copy-start.9
  144.2 3.1 %copy-start.2 = (f32[448,64]{1,0:T(8,128)S(1)}, f32[448,64]{1,0:T(8,128)}, u32[]{:S(2)}) copy-start(f32[448,64]{1,0:T(8,128)} %get-tuple-element.55) | copy-start | bytes 344068
  175.1 9.4 %copy-start.3 = (bf16[448,8,64]{2,0,1:T(8,128)(2,1)S(1)}, bf16[448,8,64]{2,0,1:T(8,128)(2,1)}, u32[]{:S(2)}) copy-start(bf16[448,8,64]{2,0,1:T(8,128)(2,1)} %get-tuple-element.42) | copy-start | bytes 1376260
  184.5 5.7 %copy-start.4 = (pred[448,960]{1,0:T(8,128)(4,1)S(1)}, pred[448,960]{1,0:T(8,128)(4,1)}, u32[]{:S(2)}) copy-start(pred[448,960]{1,0:T(8,128)(4,1)} %pad_add_fusion) | copy-start | bytes 1290244
  184.5 5.7 %copy-start.6 = (bf16[448,128]{1,0:T(8,128)(2,1)S(1)}, bf16[448,128]{1,0:T(8,128)(2,1)}, u32[]{:S(2)}) copy-start(bf16[448,128]{1,0:T(8,128)(2,1)} %slice.151) | copy-start | bytes 344068
  184.5 10.0 %slice-start = ((s8[5242880]{0:T(1024)(128)(4,1)}), s8[4194304]{0:T(1024)(128)(4,1)S(1)}, s32[]{:S(2)}) async-start(s8[5242880]{0:T(1024)(128)(4,1)} %bitcast.120), calls=%async_computation | async-start | bytes 8388608
  190.2 4.3 %slice-start.1 = ((s8[5242880]{0:T(1024)(128)(4,1)}), s8[1048576]{0:T(1024)(128)(4,1)S(1)}, s32[]{:S(2)}) async-start(s8[5242880]{0:T(1024)(128)(4,1)} %bitcast.120), calls=%async_computation.1 | async-start | bytes 2097152

commit v2 on v1

v2 whole, which is shorter than its diff:
```python
import functools

import jax
import jax.numpy as jnp
from jax import lax
from jax.experimental import pallas as pl
from jax.experimental.pallas import tpu as pltpu
from jax.sharding import PartitionSpec as P

PBLK = 64
MESH = pl.DeviceIdType.MESH
ANY = pl.BlockSpec(memory_space=pl.ANY)
VMEM = pl.BlockSpec(memory_space=pltpu.VMEM)
OFFSETS = (0, -1, 1, 2)
META = 16

epsilon = 1e-06
rope_base = 1000000.0


def place():
    rep, tp = lax.axis_index("rep"), lax.axis_index("tp")
    return lax.rem(rep // 4, 4), (tp // 2) * 2 + rep // 16, lax.rem(rep, 4), lax.rem(tp, 2)


def device_at(x, y, z, core):
    return (lax.rem(y, 2) * 16 + x * 4 + z, (y // 2) * 2 + core)


def step(value, by):
    return lax.rem(value + (by + 4), 4)


def greet(peers):
    barrier = pltpu.get_barrier_semaphore()
    for peer in peers:
        pl.semaphore_signal(barrier, inc=1, device_id=peer, device_id_type=MESH)
    pl.semaphore_wait(barrier, len(peers))


def send(source, target, send_sem, recv_sem, device):
    return pltpu.make_async_remote_copy(
        src_ref=source,
        dst_ref=target,
        send_sem=send_sem,
        recv_sem=recv_sem,
        device_id=device,
        device_id_type=MESH,
    )


class Plane:
    COPIES = 72

    def __init__(self, view, send_sems, recv_sems):
        self.view, self.ss, self.rs = view, send_sems, recv_sems
        self.x, self.y, self.z, self.core = place()
        self.started = []

    def block(self, half, first, second, part=None):
        a, b = (first, second) if half == 0 else (second, first)
        return self.view(half, step(self.x, a) * 4 + step(self.z, b), part)

    def toward(self, half, phase, sign):
        if (phase == 0) == (half == 0):
            return device_at(step(self.x, sign), self.y, self.z, self.core)
        return device_at(self.x, self.y, step(self.z, sign), self.core)

    def copy(self, half, number, ref, device):
        at = half * 36 + number
        return send(ref, ref, self.ss.at[at], self.rs.at[at], device)

    def start(self, *args):
        made = self.copy(*args)
        made.start()
        self.started.append(made)

    def sibling(self):
        return device_at(self.x, self.y, self.z, 1 - self.core)

    def share(self, half, o1, o2):
        ref = self.block(half, OFFSETS[o1], OFFSETS[o2])
        self.start(half, 20 + 4 * o1 + o2, ref, self.sibling())

    def spread(self, half, o1):
        ref = self.block(half, OFFSETS[o1], 0)
        self.start(half, 4 + 4 * o1, ref, self.toward(half, 1, 1))
        self.start(half, 5 + 4 * o1, ref, self.toward(half, 1, -1))
        self.share(half, o1, 0)

    def begin(self):
        for half in range(2):
            ref = self.block(half, 0, 0)
            self.start(half, 0, ref, self.toward(half, 0, 1))
            self.start(half, 1, ref, self.toward(half, 0, -1))
        for half in range(2):
            self.spread(half, 0)

    def arrived(self, half, number, ref):
        self.copy(half, number, ref, self.sibling()).wait_recv()

    def first(self):
        for half in range(2):
            self.arrived(half, 0, self.block(half, -1, 0))
            self.start(half, 2, self.block(half, -1, 0, 0), self.toward(half, 0, 1))
            self.arrived(half, 1, self.block(half, 1, 0))
            self.start(half, 3, self.block(half, 1, 0, 1), self.toward(half, 0, -1))
        for half in range(2):
            self.spread(half, 1)
            self.spread(half, 2)

    def opposite(self):
        for half in range(2):
            self.arrived(half, 2, self.block(half, 2, 0, 0))
            self.arrived(half, 3, self.block(half, 2, 0, 1))
            self.spread(half, 3)

    def second(self, o1):
        off, base = OFFSETS[o1], 4 + 4 * o1
        for half in range(2):
            self.arrived(half, base, self.block(half, off, -1))
            self.start(half, base + 2, self.block(half, off, -1, 0), self.toward(half, 1, 1))
            self.arrived(half, base + 1, self.block(half, off, 1))
            self.start(half, base + 3, self.block(half, off, 1, 1), self.toward(half, 1, -1))
            self.share(half, o1, 1)
            self.share(half, o1, 2)

    def second_opposite(self, o1):
        off, base = OFFSETS[o1], 4 + 4 * o1
        for half in range(2):
            self.arrived(half, base + 2, self.block(half, off, 2, 0))
            self.arrived(half, base + 3, self.block(half, off, 2, 1))
            self.share(half, o1, 3)

    def rest(self):
        yield functools.partial(self.second, 0)
        for o1 in range(1, 4):
            yield functools.partial(self.second, o1)
            yield functools.partial(self.second_opposite, o1 - 1)
        yield functools.partial(self.second_opposite, 3)

    def second_all(self):
        for act in self.rest():
            act()

    def finish(self, shared_block):
        for half in range(2):
            for o1 in range(4):
                for o2 in range(4):
                    a, b = (o1, o2) if half == 0 else (o2, o1)
                    where = step(self.x, OFFSETS[a]) * 4 + step(self.z, OFFSETS[b])
                    self.arrived(half, 20 + 4 * o1 + o2, shared_block(half, where))
        for made in self.started:
            made.wait_send()


COLUMN = tuple((dy, dc) for dy in range(4) for dc in range(2) if (dy, dc) != (0, 0))


def column_peers():
    x, y, z, core = place()
    return [device_at(x, step(y, dy), z, core if dc == 0 else 1 - core) for dy, dc in COLUMN]


def plane_peers():
    x, y, z, core = place()
    peers = [device_at(step(x, s), y, z, core) for s in (1, -1)]
    return peers + [device_at(x, y, step(z, s), core) for s in (1, -1)]


class Column:
    def __init__(self, source, target, send_sems, recv_sems, local_sem, which):
        x, y, z, core = place()
        tp = lax.axis_index("tp")
        base = which * len(COLUMN)
        self.local = pltpu.make_async_copy(
            source.at[y * 2 + core], target.at[core, lax.rem(y, 2), x * 4 + z, tp], local_sem.at[which]
        )
        self.sent, self.got = [], []
        for n, (dy, dc) in enumerate(COLUMN):
            to_y, from_y = step(y, dy), step(y, -dy)
            peer_core = core if dc == 0 else 1 - core
            sems = send_sems.at[base + n], recv_sems.at[base + n]
            to = device_at(x, to_y, z, peer_core)
            slot = target.at[peer_core, lax.rem(y, 2), x * 4 + z, tp]
            self.sent.append(send(source.at[to_y * 2 + peer_core], slot, *sems, to))
            ref = target.at[core, lax.rem(from_y, 2), x * 4 + z, (from_y // 2) * 2 + peer_core]
            self.got.append(send(ref, ref, *sems, to))

    def start(self):
        self.local.start()
        for made in self.sent:
            made.start()

    def ready(self):
        self.local.wait()
        for made in self.got:
            made.wait_recv()

    def finish(self):
        for made in self.sent:
            made.wait_send()


def viewer(target, owner):
    def view(half, where, part=None):
        if part is None:
            return target.at[owner, half, where]
        return target.at[owner, half, where, pl.ds(part * 2, 2)]

    return view


def gather_kernel(
    x_ref, win_ref, wout_ref, rows_ref, other_ref, gin_ref, gout_ref,
    a_send, a_recv, in_send, in_recv, out_send, out_recv, t_send, t_recv, p_send, p_recv, local_sem,
):
    x, y, z, core = place()
    tp = lax.axis_index("tp")
    y_lo, y_hi = lax.rem(y, 2), y // 2
    sibling = device_at(x, y, z, 1 - core)
    greet(column_peers() + plane_peers())

    inward_rows = Column(win_ref, gin_ref, a_send, a_recv, local_sem, 0)
    outward_rows = Column(wout_ref, gout_ref, a_send, a_recv, local_sem, 1)
    inward_rows.start()
    outward_rows.start()

    count, width = x_ref.shape
    cut = count // 32 * 16

    def quarter(at):
        return pl.ds(pl.multiple_of(at * width, 128), width)

    def token_copy(number, source, target, device):
        return send(source, target, t_send.at[number], t_recv.at[number], device)

    def pass_on(number, at, source=None):
        ref = other_ref.at[:, quarter(at)]
        source = rows_ref.at[:, quarter(at)] if source is None else source
        return send(source, ref, p_send.at[number], p_recv.at[number], sibling)

    home = core == y_lo
    mine = rows_ref.at[:, quarter(tp)]
    up = send(x_ref, mine, t_send.at[0], t_recv.at[core], device_at(x, step(y, 1), z, y_lo))
    down = send(x_ref, mine, t_send.at[1], t_recv.at[2 + core], device_at(x, step(y, -1), z, y_lo))
    up.start()
    down.start()

    @pl.when(home)
    def _():
        pltpu.make_async_copy(x_ref, mine, local_sem.at[2]).start()
        pass_on(0, tp, x_ref).start()

    @pl.when(jnp.logical_not(home))
    def _():
        token_copy(4, x_ref, mine, sibling).start()
        pltpu.make_async_copy(x_ref, other_ref.at[:, quarter(tp)], local_sem.at[2]).start()

    inward = Plane(viewer(gin_ref, core), in_send, in_recv)
    outward = Plane(viewer(gout_ref, core), out_send, out_recv)
    inward_rows.ready()
    inward.begin()
    inward.first()
    inward.opposite()
    outward_rows.ready()
    outward.begin()

    def away_blocks():
        below, above = step(y, -1), step(y, 1)
        for k in range(2):
            low = (below // 2) * 2 + k
            high = (above // 2) * 2 + k
            yield k, low, high, below, above

    @pl.when(jnp.logical_not(home))
    def _():
        for k, low, high, below, above in away_blocks():
            ref = rows_ref.at[:, quarter(low)]
            token_copy(k, ref, ref, sibling).wait_recv()
            ref = rows_ref.at[pl.ds(0, cut), quarter(low)]
            token_copy(5 + k, ref, ref, device_at(x, above, z, core)).start()
            ref = rows_ref.at[:, quarter(high)]
            token_copy(2 + k, ref, ref, sibling).wait_recv()
            ref = rows_ref.at[pl.ds(cut, count - cut), quarter(high)]
            token_copy(7 + k, ref, ref, device_at(x, below, z, core)).start()
            pass_on(k, low).start()
            pass_on(2 + k, high).start()

    inward.second_all()
    outward.first()
    outward.opposite()
    outward.second_all()

    @pl.when(jnp.logical_not(home))
    def _():
        for k, low, high, below, above in away_blocks():
            ref = rows_ref.at[pl.ds(0, cut), quarter(low)]
            token_copy(5 + k, ref, ref, sibling).wait_send()
            ref = rows_ref.at[pl.ds(cut, count - cut), quarter(high)]
            token_copy(7 + k, ref, ref, sibling).wait_send()
            pass_on(k, low).wait_send()
            pass_on(2 + k, high).wait_send()
        token_copy(4, x_ref, mine, sibling).wait_send()
        pltpu.make_async_copy(x_ref, other_ref.at[:, quarter(tp)], local_sem.at[2]).wait()
        for number in (0, 2, 3):
            pass_on(number, tp).wait_recv()

    @pl.when(home)
    def _():
        opposite = 1 - y_hi
        for k in range(2):
            at = quarter(opposite * 2 + k)
            ref = rows_ref.at[pl.ds(0, cut), at]
            token_copy(5 + k, ref, ref, sibling).wait_recv()
            ref = rows_ref.at[pl.ds(cut, count - cut), at]
            token_copy(7 + k, ref, ref, sibling).wait_recv()
            pass_on(2 + k, opposite * 2 + k).start()
        ref = rows_ref.at[:, quarter(y_hi * 2 + 1 - core)]
        token_copy(4, ref, ref, sibling).wait_recv()
        pltpu.make_async_copy(x_ref, mine, local_sem.at[2]).wait()
        for number in range(4):
            pass_on(number, tp).wait_recv()
        pass_on(0, tp, x_ref).wait_send()
        for k in range(2):
            pass_on(2 + k, tp).wait_send()

    up.wait_send()
    down.wait_send()
    inward_rows.finish()
    outward_rows.finish()
    inward.finish(viewer(gin_ref, 1 - core))
    outward.finish(viewer(gout_ref, 1 - core))


def gather_all(rows, win, wout):
    count, width = rows.shape
    sems = [14, 14, Plane.COPIES, Plane.COPIES, Plane.COPIES, Plane.COPIES, 9, 9, 4, 4, 3]
    return pl.pallas_call(
        gather_kernel,
        name="gather_all",
        out_shape=(
            jax.ShapeDtypeStruct((count, 4 * width), rows.dtype),
            jax.ShapeDtypeStruct((count, 4 * width), rows.dtype),
            jax.ShapeDtypeStruct((2, 2, 16, 4) + win.shape[1:], win.dtype),
            jax.ShapeDtypeStruct((2, 2, 16, 4) + wout.shape[1:], wout.dtype),
        ),
        in_specs=[ANY] * 3,
        out_specs=(ANY,) * 4,
        scratch_shapes=[pltpu.SemaphoreType.DMA((n,)) for n in sems],
        compiler_params=pltpu.CompilerParams(collective_id=0, has_side_effects=True),
    )(rows, win, wout)


TILE = 64


def attend_kernel(
    q_ref, own_ref, prompt_ref, bounds_ref, group_ref, wout_ref, out_ref, gout_ref,
    prompts, shared, total, sums, a_send, a_recv, out_send, out_recv, kv_send, kv_recv, local_sem,
):
    x, y, z, core = place()
    head = prompt_ref.shape[1] // 2
    heads = q_ref.shape[0]
    greet(column_peers() + plane_peers())
    mine = pltpu.make_async_copy(prompt_ref, prompts.at[core * 16 + x * 4 + z], local_sem.at[1])
    mine.start()
    rows = Column(wout_ref, gout_ref, a_send, a_recv, local_sem, 0)
    rows.start()
    mine.wait()

    def prompt_viewer(owner):
        def view(half, where, part=None):
            span = pl.ds(half * 64, 64) if part is None else pl.ds(half * 64 + part * 32, 32)
            return prompts.at[owner * 16 + where, span]

        return view

    kv = Plane(prompt_viewer(core), kv_send, kv_recv)
    outward = Plane(viewer(gout_ref, core), out_send, out_recv)
    kv.begin()
    scale = head ** (-0.5) * 1.4426950408889634

    def weigh(tile, keys, values, low, high):
        span = pl.ds(tile * TILE, TILE)
        queries = q_ref[:, span].reshape(heads * TILE, head)
        scores = lax.dot_general(
            queries, keys, (((1,), (1,)), ((), ())), preferred_element_type=jnp.float32
        )
        count = keys.shape[0]
        at = lax.broadcasted_iota(jnp.int32, (TILE, count), 1)
        allowed = (at >= low) & (at < high)
        weights = jnp.where(
            allowed[None], jnp.exp2(scores.reshape(heads, TILE, count) * scale), 0.0
        )
        blend = jnp.dot(
            weights.astype(jnp.bfloat16).reshape(heads * TILE, count), values,
            preferred_element_type=jnp.float32,
        )
        return span, jnp.sum(weights, axis=-1, keepdims=True), blend.reshape(heads, TILE, head)

    def own_tile(tile):
        span = slice(tile * TILE, (tile + 1) * TILE)
        count = min(-(-(tile + 1) * TILE // 128) * 128, own_ref.shape[0])
        low = bounds_ref[span, 0:1]
        high = lax.broadcasted_iota(jnp.int32, (TILE, 1), 0) + (tile * TILE + 1)
        span, weight, blend = weigh(tile, own_ref[:count, :head], own_ref[:count, head:], low, high)
        total[:, span] = blend
        sums[:, span] = jnp.broadcast_to(weight, (heads, TILE, head))

    def shared_tile(tile):
        span = slice(tile * TILE, (tile + 1) * TILE)
        low, high = bounds_ref[span, 1:2], bounds_ref[span, 2:3]
        span, weight, blend = weigh(tile, shared[:, :head], shared[:, head:], low, high)
        blend = (total[:, span] + blend) / (sums[:, span] + weight)
        for h in range(heads):
            out_ref[span, h * head : (h + 1) * head] = blend[h].astype(jnp.bfloat16)

    tiles = q_ref.shape[1] // TILE
    for tile in range(4):
        own_tile(tile)
    rows.ready()
    kv.first()
    outward.begin()
    own_tile(4)
    kv.opposite()
    own_tile(5)
    kv.second(0)
    outward.first()
    own_tile(6)
    acts = list(kv.rest())[1:]
    for act in acts[:3]:
        act()
    outward.opposite()
    for act in acts[3:]:
        act()
    kv.finish(prompt_viewer(1 - core))
    for j in range(group_ref.shape[0]):
        shared[j * prompts.shape[1] : (j + 1) * prompts.shape[1]] = prompts[group_ref[j]]
    later = list(outward.rest())
    for tile in range(tiles):
        later[tile]()
        shared_tile(tile)
    for act in later[tiles:]:
        act()
    rows.finish()
    outward.finish(viewer(gout_ref, 1 - core))


def attend(queries, own, prompt, bounds, group, wout):
    heads, count, head = queries.shape
    sems = [7, 7, Plane.COPIES, Plane.COPIES, Plane.COPIES, Plane.COPIES, 2]
    return pl.pallas_call(
        attend_kernel,
        name="attend",
        out_shape=(
            jax.ShapeDtypeStruct((count, heads * head), jnp.bfloat16),
            jax.ShapeDtypeStruct((2, 2, 16, 4) + wout.shape[1:], wout.dtype),
        ),
        in_specs=[VMEM] * 4 + [pl.BlockSpec(memory_space=pltpu.SMEM), ANY],
        out_specs=(VMEM, ANY),
        scratch_shapes=[
            pltpu.VMEM((32,) + prompt.shape, prompt.dtype),
            pltpu.VMEM((group.shape[0] * prompt.shape[0], prompt.shape[1]), prompt.dtype),
            pltpu.VMEM(queries.shape, jnp.float32),
            pltpu.VMEM(queries.shape, jnp.float32),
        ]
        + [pltpu.SemaphoreType.DMA((n,)) for n in sems],
        compiler_params=pltpu.CompilerParams(
            collective_id=1, has_side_effects=True, vmem_limit_bytes=48 * 2**20
        ),
    )(queries, own, prompt, bounds, group, wout)


BLOCK = 128
LEVELS = ("z1", "x1", "z2", "x2")


def level_bits(shift, sign):
    odd = shift % 2 == 1
    far = (shift >= 2) if sign == 1 else ((shift == 1) | (shift == 2))
    return odd, far


def along_z(shift, z):
    return shift % 4, shift // 4 + (z < shift % 4).astype(jnp.int32)


def y_shift(shift, x, z):
    shift_z, need_x = along_z(shift, (z + shift) % 4)
    end_x = (x + need_x) % 4
    return (need_x // 4 + (end_x < need_x % 4).astype(jnp.int32)) % 2 == 1


def move_masks(shift, x, z):
    masks = []
    for sign in (1, -1):
        odd_z, far_z = level_bits(shift % 4, sign)
        for level in LEVELS:
            end_z = (z + (2 * far_z.astype(jnp.int32) if level in ("z1", "x1") else 0)) % 4
            odd_x, far_x = level_bits(along_z(shift, end_z)[1] % 4, sign)
            masks.append({"z1": odd_z, "x1": odd_x, "z2": far_z, "x2": far_x}[level])
    masks = jnp.stack(masks).astype(jnp.float32)
    return jnp.broadcast_to(masks[:, :, None], masks.shape + (BLOCK,))


def return_kernel(
    blend_ref, w0_ref, w1_ref, residual_ref, mask_ref, out_ref,
    sums, source, home_sum, home_got, raw, final, held, landed,
    src_send, raw_recv, fin_recv, move_send, move_recv,
):
    x, y, z, core = place()
    y_lo, y_hi = lax.rem(y, 2), y // 2
    width = out_ref.shape[1]
    blocks = width // BLOCK
    above, below = step(y, 1), step(y, -1)
    sibling = device_at(x, y, z, 1 - core)
    peers = [device_at(x, at, z, k) for at in (above, below) for k in range(2)] + [sibling]
    peers += [device_at(step(x, s), y, z, core) for s in (1, -1, 2)]
    peers += [device_at(x, y, step(z, s), core) for s in (1, -1, 2)]
    greet(peers)
    home = core == y_lo
    away = jnp.logical_not(home)

    far, up, down = 1 - y_hi, above // 2, below // 2
    quarters = (
        jnp.where(home, far * 2, up * 2),
        jnp.where(home, far * 2 + 1, down * 2 + 1),
        jnp.where(home, y_hi * 2 + 1 - core, up * 2 + 1),
        jnp.where(home, y_hi * 2 + core, down * 2),
    )
    pieces = w0_ref.shape[0]
    depth = w0_ref.shape[2]

    def raw_copy(j, slot):
        to = device_at(x, (above, below)[slot], z, core)
        at = slot * blocks + j
        return send(source.at[slot, j], raw.at[slot, j], src_send.at[at], raw_recv.at[at], to)

    def sibling_copy(j):
        at = 2 * blocks + j
        return send(home_sum.at[j], home_got.at[j], src_send.at[at], fin_recv.at[at], sibling)

    def final_copy(j, at):
        slot, k = ((0, 0), (1, 1), (0, 1), (1, 0))[at]
        to = device_at(x, (above, below)[slot], z, k)
        return send(
            source.at[at, j], final.at[slot, j],
            src_send.at[at * blocks + j], fin_recv.at[slot * blocks + j], to,
        )

    def multiply(pair):
        for at in range(4):
            start = pl.multiple_of(quarters[at] * width + pair * 2 * BLOCK, 2 * BLOCK)
            total = None
            for half in range(pieces):
                for n, w_ref in enumerate((w0_ref, w1_ref)):
                    column = (half * 2 + n) * depth
                    term = lax.dot_general(
                        blend_ref[:, column : column + depth], w_ref[half, pl.ds(start, 2 * BLOCK)],
                        (((1,), (1,)), ((), ())), preferred_element_type=jnp.float32,
                    )
                    total = term if total is None else total + term
            sums[at] = total
        lanes = [pl.ds(i * BLOCK, BLOCK) for i in range(2)]

        @pl.when(home)
        def _():
            for i in range(2):
                j = pair * 2 + i
                for slot in range(2):
                    source[slot, j] = sums[slot, :, lanes[i]].astype(jnp.bfloat16)
                    raw_copy(j, slot).start()
            for i in range(2):
                j = pair * 2 + i
                theirs = pl.ds(pl.multiple_of((1 - core) * width + j * BLOCK, BLOCK), BLOCK)
                home_sum[j] = sums[2, :, lanes[i]] + residual_ref[:, theirs].astype(jnp.float32)
                sibling_copy(j).start()
                mine = pl.ds(pl.multiple_of(core * width + j * BLOCK, BLOCK), BLOCK)
                home_got[j] = sums[3, :, lanes[i]] + residual_ref[:, mine].astype(jnp.float32)

        @pl.when(away)
        def _():
            for i in range(2):
                j = pair * 2 + i
                for at in (2, 3):
                    source[at, j] = sums[at, :, lanes[i]].astype(jnp.bfloat16)
                    final_copy(j, at).start()
            for i in range(2):
                j = pair * 2 + i
                for at in range(2):
                    partial[at, j] = sums[at, :, lanes[i]].astype(jnp.bfloat16)

    partial = source

    def add(j):
        @pl.when(away)
        def _():
            for slot in range(2):
                raw_copy(j, slot).wait_recv()
                source[slot, j] = (
                    partial[slot, j].astype(jnp.float32) + raw[slot, j].astype(jnp.float32)
                ).astype(jnp.bfloat16)
                final_copy(j, slot).start()

    def move(j, level):
        by = (1, -1)[j % 2] if LEVELS[level][1] == "1" else 2
        if LEVELS[level][0] == "z":
            to = device_at(x, y, step(z, by), core)
        else:
            to = device_at(step(x, by), y, z, core)
        at = level * blocks + j
        return send(
            held.at[level, j], landed.at[level, j], move_send.at[at], move_recv.at[at], to
        )

    def finish(j):
        for slot in range(2):
            final_copy(j, slot).wait_recv()

        @pl.when(away)
        def _():
            sibling_copy(j).wait_recv()

        total = final[0, j].astype(jnp.float32) + final[1, j].astype(jnp.float32) + home_got[j]
        held[0, j] = total.astype(jnp.bfloat16)
        move(j, 0).start()

    def take(j, level):
        move(j, level).wait_recv()
        chosen = jnp.where(
            mask_ref[(j % 2) * len(LEVELS) + level] > 0.5,
            landed[level, j].astype(jnp.float32),
            held[level, j].astype(jnp.float32),
        ).astype(jnp.bfloat16)
        if level + 1 < len(LEVELS):
            held[level + 1, j] = chosen
            move(j, level + 1).start()
        else:
            out_ref[:, j * BLOCK : (j + 1) * BLOCK] = chosen

    for tick in range(blocks + 2 + len(LEVELS)):
        if tick < blocks // 2:
            multiply(tick)
        for j in range(blocks):
            if tick == j + 1:
                add(j)
        for j in range(blocks):
            if tick == j + 2:
                finish(j)
        for level in reversed(range(len(LEVELS))):
            j = tick - 3 - level
            if 0 <= j < blocks:
                take(j, level)

    for j in range(blocks):
        for level in range(len(LEVELS)):
            move(j, level).wait_send()

        @pl.when(home)
        def _():
            raw_copy(j, 0).wait_send()
            raw_copy(j, 1).wait_send()
            sibling_copy(j).wait_send()

        @pl.when(away)
        def _():
            for at in range(4):
                final_copy(j, at).wait_send()


def return_rows(blended, w0, w1, residual, masks):
    count = blended.shape[0]
    width = residual.shape[1] // 2
    blocks = width // BLOCK
    levels = len(LEVELS)

    def room(n, dtype=jnp.bfloat16):
        return pltpu.VMEM((n, blocks, count, BLOCK), dtype)

    return pl.pallas_call(
        return_kernel,
        name="return_rows",
        out_shape=jax.ShapeDtypeStruct((count, width), jnp.bfloat16),
        in_specs=[VMEM] * 5,
        out_specs=VMEM,
        scratch_shapes=[
            pltpu.VMEM((4, count, 2 * BLOCK), jnp.float32),
            room(4),
            pltpu.VMEM((blocks, count, BLOCK), jnp.float32),
            pltpu.VMEM((blocks, count, BLOCK), jnp.float32),
            room(2),
            room(2),
            room(levels),
            room(levels),
        ]
        + [pltpu.SemaphoreType.DMA((n * blocks,)) for n in (4, 2, 3, levels, levels)],
        compiler_params=pltpu.CompilerParams(
            collective_id=2, has_side_effects=True, vmem_limit_bytes=56 * 2**20
        ),
    )(blended, w0, w1, residual, masks)


def rms_rows(values, gain_row):
    floats = values.astype(jnp.float32)
    scaled = lax.rsqrt(jnp.mean(floats * floats, axis=-1, keepdims=True) + epsilon)
    return floats * scaled * gain_row


def rotary(values, positions):
    half_size = values.shape[-1] // 2
    spread = jnp.arange(half_size, dtype=jnp.float32) * (2.0 / values.shape[-1])
    frequency = rope_base ** (-spread)
    angles = positions.astype(jnp.float32)[:, None] * frequency[None, :]
    cosine = jnp.cos(angles)[:, None, :]
    sine_part = jnp.sin(angles)[:, None, :]
    front_half = values[..., :half_size]
    back_half = values[..., half_size:]
    return jnp.concatenate(
        [front_half * cosine - back_half * sine_part, back_half * cosine + front_half * sine_part],
        axis=-1,
    )


def slot_layout(seq_lengths, row_count):
    ends_at = jnp.cumsum(seq_lengths)
    starts_at = ends_at - seq_lengths
    position = jnp.arange(row_count, dtype=jnp.int32)
    slot_of = jnp.sum((position[:, None] >= ends_at[None, :]).astype(jnp.int32), axis=1)
    onehot = (
        slot_of[:, None] == jnp.arange(seq_lengths.shape[0], dtype=jnp.int32)[None, :]
    ).astype(jnp.int32)
    within = position - jnp.sum(onehot * starts_at[None, :], axis=1)
    return (slot_of, within, onehot)


def shards(
    tokens,
    prompt_rows,
    norm_gain,
    w_query,
    w_key,
    w_value,
    w_out,
    q_gain,
    k_gain,
    seq_lengths,
    prompt_group,
    prompt_blocks,
    dest_offset,
):
    row_count, width = tokens.shape
    prompt_len = prompt_rows.shape[0]
    head_size = q_gain.shape[0]
    slot_count = seq_lengths.shape[0]
    depth = w_query.shape[0]
    groups = w_key.shape[1] // head_size
    rep = lax.axis_index("rep")

    halves = w_query.astype(jnp.bfloat16).reshape(depth, groups, 2, -1)
    key_cols = w_key.astype(jnp.bfloat16).reshape(depth, groups, 1, head_size)
    value_cols = w_value.astype(jnp.bfloat16).reshape(depth, groups, 1, head_size)
    win = jnp.concatenate([halves, jnp.concatenate([key_cols, value_cols], axis=2)], axis=3)
    win = win.transpose(1, 2, 0, 3).reshape(2 * groups, depth, -1)
    wout = w_out.astype(jnp.bfloat16).reshape(2 * groups, 2, -1, depth).transpose(1, 0, 3, 2)
    meta = jnp.concatenate([prompt_group, prompt_blocks]).astype(jnp.bfloat16)
    meta = jnp.pad(meta[None, :], ((0, META - 1), (0, width - 2 * slot_count)))
    rows, other, gin, gout = gather_all(
        jnp.concatenate([tokens, prompt_rows, meta], axis=0), win, wout[0]
    )

    plane_x, plane_z = rep // 4 % 4, rep % 4
    slot_of, within, onehot = slot_layout(seq_lengths, row_count)
    crosses = y_shift(dest_offset, plane_x, plane_z)
    pair = jnp.stack([rows[row_count + prompt_len], other[row_count + prompt_len]])
    pair = pair[:, : 2 * slot_count].astype(jnp.int32).reshape(2, 2, slot_count)
    group_here, blocks_here = jnp.where(crosses, pair[1], pair[0])
    shift_rows = jnp.sum(onehot * dest_offset[None, :], axis=1)
    row_crosses = jnp.sum(onehot * crosses[None, :], axis=1) == 1
    inputs = jnp.where(row_crosses[:, None], other[:row_count], rows[:row_count])
    normed = rms_rows(
        jnp.concatenate([inputs, rows[row_count : row_count + prompt_len]], axis=0), norm_gain
    ).astype(jnp.bfloat16)
    features = normed.shape[1]
    gin = gin.reshape(2, features, -1)
    left = jnp.dot(normed, gin[0], preferred_element_type=jnp.float32)
    right = jnp.dot(normed, gin[1], preferred_element_type=jnp.float32)
    half_width = left.shape[1] - head_size
    query_sum = jnp.concatenate([left[:row_count, :half_width], right[:row_count, :half_width]], axis=1)
    key_sum, values_all = left[:, half_width:], right[:, half_width:].astype(jnp.bfloat16)
    q_heads = query_sum.shape[1] // head_size

    prefix_len = jnp.sum(onehot * (blocks_here * PBLK)[None, :], axis=1)
    positions = prefix_len + within
    queries = rotary(rms_rows(query_sum.reshape(row_count, q_heads, head_size), q_gain), positions)
    queries = queries.astype(jnp.bfloat16).transpose(1, 0, 2)
    all_positions = jnp.concatenate([positions, jnp.arange(prompt_len, dtype=jnp.int32)])
    keys_all = rotary(rms_rows(key_sum[:, None], k_gain), all_positions).astype(jnp.bfloat16)[:, 0]
    pairs = jnp.concatenate([keys_all, values_all], axis=1)
    bounds = jnp.stack(
        [jnp.arange(row_count, dtype=jnp.int32) - within, slot_of * prompt_len, slot_of * prompt_len + prefix_len], axis=1
    )
    bounds = jnp.pad(bounds, ((0, 0), (0, head_size - 3)))
    blended, gout_b = attend(
        queries, pairs[:row_count], pairs[row_count:], bounds, group_here, wout[1]
    )
    gout, gout_b = gout.reshape(2, features, -1), gout_b.reshape(2, features, -1)
    residual = lax.dynamic_slice_in_dim(
        inputs, lax.axis_index("tp") // 2 * (2 * width), 2 * width, axis=1
    )
    return return_rows(
        blended, gout, gout_b, residual,
        move_masks(shift_rows, plane_x, plane_z),
    )


def solution(mesh):
    return jax.shard_map(
        shards,
        mesh=mesh,
        in_specs=(
            P("rep", "tp"),
            P("rep", "tp"),
            P(),
            P(("rep", "tp"), None),
            P(("rep", "tp"), None),
            P(("rep", "tp"), None),
            P(None, ("rep", "tp")),
            P(),
            P(),
            P(),
            P("rep"),
            P("rep"),
            P(),
        ),
        out_specs=P("rep", "tp"),
        check_vma=False,
    )
```

time: 307 us -> 270 us (0.88); the launches traced: 301 us -> 268 us
  matrix products: 34.3 us -> 9.72 us
  Pallas kernels: 204 us -> 219 us
  other arithmetic: 27.5 us -> 17.8 us
  between operations: 7.85 us -> 0.49 us
  local copies, waits for them, and re-layouts: 27.9 us -> 20.6 us
    dot_general x4 -> x0, matrix products: 19.6 us -> none  [the longest x1 7.34 us: shards(): lax.dot_general(blended[:, half_rows:], gout[1], (((1,), (1,)), ((), ()))...]
    pallas_call x1, Pallas kernels: 24.8 us -> 41.4 us  [attend(): pl.pallas_call(attend_kernel, name='attend', out_shape=(jax.ShapeDtypeStr...]
    slice x5 -> x6, local copies, waits for them, and re-layouts: 12.3 us -> 4.23 us  [the longest x1 2.37 us: shards(): rows[row_count:row_count + prompt_len]]
    pallas_call x1, Pallas kernels: 83.2 us -> 75.7 us  [gather_all(): pl.pallas_call(gather_kernel, name='gather_all', out_shape=(jax.ShapeDtyp...]
    pallas_call x1, Pallas kernels: 95.9 us -> 102 us  [return_rows(): pl.pallas_call(return_kernel, name='return_rows', out_shape=jax.ShapeDtyp...]
    slice x1, local copies, waits for them, and re-layouts: 9.83 us -> 5.64 us  [shards(): left = jnp.dot(normed, gin[0], preferred_element_type=jnp.float32)]
    dot_general x1, matrix products: 8.99 us -> 4.82 us  [shards(): left = jnp.dot(normed, gin[0], preferred_element_type=jnp.float32)]
    another operation x15 -> x4, other arithmetic: 5.02 us -> 0.9 us
where the time goes in v2:
time: 270 us; the launch traced here: 268 us
  Pallas kernels  219 us (81%)
  local copies, waits for them, and re-layouts  20.6 us (8%)
  other arithmetic  17.8 us (7%)
  matrix products  9.72 us (4%)
    pallas_call x1, Pallas kernels, return_rows(): pl.pallas_call(return_kernel, name='return_rows', out_shape=jax.ShapeDtyp...  102 us
    pallas_call x1, Pallas kernels, gather_all(): pl.pallas_call(gather_kernel, name='gather_all', out_shape=(jax.ShapeDtyp...  75.7 us
    pallas_call x1, Pallas kernels, attend(): pl.pallas_call(attend_kernel, name='attend', out_shape=(jax.ShapeDtypeStr...  41.4 us
    slice x1, local copies, waits for them, and re-layouts, shards(): left = jnp.dot(normed, gin[0], preferred_element_type=jnp.float32)  5.64 us

profile of v2, /device:TPU:16, one launch (start us, length us, event | category | flops | bytes accessed | tf_op | source)
XLA Modules:
  0.0 268.0 jit_solution(15665447794735867727)
XLA Ops:
  0.0 0.0 copy-start.2
  0.0 0.8 fusion.48
  0.8 0.7 convert_bitcast_fusion
  1.5 0.1 fusion.21
  1.6 2.6 pad_maximum_fusion.2.x_ref
  4.2 1.1 convert_element_type.124
  5.3 0.2 reshape.829
  5.5 0.1 copy.51
  5.7 0.7 slice_bitcast_fusion
  6.3 0.0 copy-done.2
  6.4 0.2 reshape.825
  6.6 0.1 copy.42
  6.7 0.0 copy-done.3
  6.8 0.0 copy-done.4
  6.9 0.8 maximum_maximum_fusion
  7.6 75.7 %gather_all.1 = (bf16[592,5120]{1,0:T(8,128)(2,1)}, bf16[592,5120]{1,0:T(8,128)(2,1)}, bf16[2,2,16,4,40,640]{5,4,3,2,1,0:T(8,128)(2,1)}, bf16[2,2,16,4,40,256]{5,4,3,2,1,0:T(8,128)(2,1)}) custom-call(bf16[592,1280]{1,0:T(8,128)(2,1)} %pad_maximum_fusion.2.x_ref, bf16[8,40,640]{2,1,0:T(8,128)(2,1)} %bitcast.55, bf16[8,40,256]{2,1,0:T(8,128)(2,1)} %get-tuple-element.38.wout_ref), custom_call_target="tpu_custom_call" | custom-call | tf_op jit(solution)/shard_map/gather_all/pallas_call | solution.py:339
  83.4 0.9 slice.80
  84.3 0.9 slice.81
  85.2 0.1 squeeze.22
  85.3 0.1 squeeze.23
  85.4 0.0 copy-done.9
  85.4 0.2 reduce-window.8
  85.6 0.1 convert_reduce_fusion
  85.7 0.0 copy-done.5
  85.7 0.1 select_reduce_fusion
  85.9 0.1 compare_or_fusion.1
  86.0 1.8 broadcast_in_dim.13.mask_ref
  87.8 0.1 copy.46
  88.0 4.0 %slice_select_fusion = bf16[448,5120]{1,0:T(8,128)(2,1)S(1)} fusion(bf16[592,5120]{1,0:T(8,128)(2,1)} %get-tuple-element.12, bf16[592,5120]{1,0:T(8,128)(2,1)} %get-tuple-element.11, pred[448]{0:T(512)(128)(4,1)S(1)} %broadcast_compare_fusion.2), kind=kLoop, calls=%fused_computation.6 | loop fusion | flops 2293760 | bytes 13763008 | tf_op jit(solution)/shard_map/jit(_where)/select_n | solution.py:780
  92.0 0.0 copy-start.1
  92.0 2.4 slice.74
  94.4 1.2 fusion
  95.7 0.0 copy-start.8
  95.7 5.6 %fusion.50 = (bf16[1,2,16,4,40,640]{5,4,3,2,1,0:T(8,128)(2,1)S(1)}, bf16[1,2,16,4,40,640]{5,4,3,2,1,0:T(8,128)(2,1)S(1)}) fusion(bf16[2,2,16,4,40,640]{5,4,3,2,1,0:T(8,128)(2,1)} %get-tuple-element.13), kind=kLoop, calls=%fused_computation.157 | loop fusion | bytes 26214400 | tf_op jit(solution)/shard_map/slice | solution.py:786
  101.3 0.0 copy-done.8
  101.3 0.0 copy-start.6
  101.4 4.8 %fusion.45 = f32[576,640]{1,0:T(8,128)S(1)} fusion(bf16[5120,640]{1,0:T(8,128)(2,1)S(1)} %bitcast.52, f32[5120]{0:T(1024)S(1)} %copy-done.8, f32[576]{0:T(1024)S(1)} %add_rsqrt_fusion.2, bf16[128,5120]{1,0:T(8,128)(2,1)S(1)} %slice.74, bf16[448,5120]{1,0:T(8,128)(2,1)S(1)} %slice_select_fusion), kind=kOutput, calls=%fused_computation.154 | convolution fusion | flops 3795517440 | bytes 13949184 | tf_op jit(solution)/shard_map/dot_general | solution.py:786
  106.2 0.2 multiply_reduce_fusion.1
  106.4 0.0 copy-done.6
  106.4 0.1 multiply_bitcast_fusion
  106.5 0.1 add_convert_fusion.1
  106.6 1.5 fusion.15
  108.2 0.0 copy-done.1
  108.2 4.9 %fusion.43 = f32[576,640]{1,0:T(8,128)S(1)} fusion(bf16[5120,640]{1,0:T(8,128)(2,1)S(1)} %bitcast.51, f32[5120]{0:T(1024)S(1)} %copy-done.8, f32[576]{0:T(1024)S(1)} %add_rsqrt_fusion.2, bf16[128,5120]{1,0:T(8,128)(2,1)S(1)} %slice.74, bf16[448,5120]{1,0:T(8,128)(2,1)S(1)} %slice_select_fusion), kind=kOutput, calls=%fused_computation.153 | convolution fusion | flops 3795517440 | bytes 13949184 | tf_op jit(solution)/shard_map/dot_general | solution.py:787
  113.1 0.1 pad_maximum_fusion.4.prompt_ref
  113.2 0.2 pad_maximum_fusion.3
  113.4 0.9 multiply_cosine_fusion.1
  114.3 0.1 slice.94
  114.4 0.1 slice.95
  114.5 0.0 copy-start.7
  114.5 0.5 fusion.5
  115.0 0.4 copy.48
  115.4 0.5 multiply_reduce_fusion
  115.9 0.1 copy.44
  116.0 0.0 copy-done.7
  116.1 0.5 fusion.3
  116.6 0.7 subtract_convert_fusion
  117.3 0.5 maximum_bitcast_fusion.q_ref
  117.8 41.4 %attend.1 = (bf16[448,1024]{1,0:T(8,128)(2,1)S(1)}, bf16[2,2,16,4,40,256]{5,4,3,2,1,0:T(8,128)(2,1)}) custom-call(bf16[8,448,128]{2,1,0:T(8,128)(2,1)S(1)} %maximum_bitcast_fusion.q_ref, bf16[448,256]{1,0:T(8,128)(2,1)S(1)} %slice.102.own_ref, bf16[128,256]{1,0:T(8,128)(2,1)S(1)} %pad_maximum_fusion.4.prompt_ref, s32[448,128]{1,0:T(8,128)S(1)} %pad.9.bounds_ref, ...), custom_call_target="tpu_custom_call" | custom-call | tf_op jit(solution)/shard_map/attend/pallas_call | solution.py:453
  159.3 0.0 copy-start
  159.3 0.9 copy-done
  160.2 3.2 %constant_dynamic-slice_fusion.residual_ref = bf16[448,2560]{1,0:T(8,128)(2,1)} fusion(bf16[448,5120]{1,0:T(8,128)(2,1)} %copy-done.1, s32[]{:T(128)S(6)} %select_n.290), kind=kLoop, calls=%fused_computation.151 | loop fusion | bytes 4587524 | tf_op jit(solution)/shard_map/dynamic_slice | solution.py:808
  163.4 102.3 %return_rows.1 = bf16[448,1280]{1,0:T(8,128)(2,1)} custom-call(bf16[448,1024]{1,0:T(8,128)(2,1)} %copy-done, bf16[2,5120,256]{2,1,0:T(8,128)(2,1)} %bitcast.53, bf16[2,5120,256]{2,1,0:T(8,128)(2,1)} %bitcast.54, bf16[448,2560]{1,0:T(8,128)(2,1)} %constant_dynamic-slice_fusion.residual_ref, f32[8,448,128]{2,1,0:T(8,128)} %broadcast_in_dim.13.mask_ref), custom_call_target="tpu_custom_call" | custom-call | tf_op jit(solution)/shard_map/return_rows/pallas_call | solution.py:681
  265.7 2.3 copy.53
  (34 shorter events, 0.4 us)
Async XLA Ops:
  0.0 6.3 %copy-start.2 = (f32[40,4096]{1,0:T(8,128)S(1)}, f32[40,4096]{1,0:T(8,128)}, u32[]{:S(2)}) copy-start(f32[40,4096]{1,0:T(8,128)} %param.16) | copy-start | bytes 1966084
  0.0 6.7 %copy-start.3 = (f32[40,512]{1,0:T(8,128)S(1)}, f32[40,512]{1,0:T(8,128)}, u32[]{:S(2)}) copy-start(f32[40,512]{1,0:T(8,128)} %param.17) | copy-start | bytes 245764
  0.0 6.8 %copy-start.4 = (f32[40,512]{1,0:T(8,128)S(1)}, f32[40,512]{1,0:T(8,128)}, u32[]{:S(2)}) copy-start(f32[40,512]{1,0:T(8,128)} %param.18) | copy-start | bytes 245764
  4.2 81.3 %copy-start.9 = (s32[4]{0:T(128)S(1)}, s32[4]{0:T(128)}, u32[]{:S(2)}) copy-start(s32[4]{0:T(128)} %param.22) | copy-start | bytes 52
  4.2 81.5 %copy-start.5 = (s32[4]{0:T(128)S(1)}, s32[4]{0:T(128)}, u32[]{:S(2)}) copy-start(s32[4]{0:T(128)} %param.25) | copy-start | bytes 52
  92.0 16.1 %copy-start.1 = (bf16[448,5120]{1,0:T(8,128)(2,1)}, bf16[448,5120]{1,0:T(8,128)(2,1)S(1)}, u32[]{:S(2)}) copy-start(bf16[448,5120]{1,0:T(8,128)(2,1)S(1)} %slice_select_fusion) | copy-start | bytes 13762564
  95.7 5.7 %copy-start.8 = (f32[5120]{0:T(1024)S(1)}, f32[5120]{0:T(1024)}, u32[]{:S(2)}) copy-start(f32[5120]{0:T(1024)} %param.15) | copy-start | bytes 61444
  101.3 5.0 %copy-start.6 = (f32[128]{0:T(128)S(1)}, f32[128]{0:T(128)}, u32[]{:S(2)}) copy-start(f32[128]{0:T(128)} %param.21) | copy-start | bytes 1540
  114.5 1.6 copy-start.7
  159.3 0.9 copy-start

commit v3 on v2

--- a/solution.py
+++ b/solution.py
@@ -2,17 +2,21 @@
 
 import jax
 import jax.numpy as jnp
+import numpy as np
 from jax import lax
 from jax.experimental import pallas as pl
 from jax.experimental.pallas import tpu as pltpu
 from jax.sharding import PartitionSpec as P
 
 PBLK = 64
+PBLOCKS = 2
 MESH = pl.DeviceIdType.MESH
 ANY = pl.BlockSpec(memory_space=pl.ANY)
 VMEM = pl.BlockSpec(memory_space=pltpu.VMEM)
 OFFSETS = (0, -1, 1, 2)
 META = 16
+CROSS, START, PROMPT, SLOT, WITHIN, MOVES = 0, 1, 2, 3, 4, 8
+EARLY = 128
 
 epsilon = 1e-06
 rope_base = 1000000.0
@@ -169,22 +173,22 @@
 
 
 class Column:
-    def __init__(self, source, target, send_sems, recv_sems, local_sem, which):
+    def __init__(self, source, land, send_sems, recv_sems, local_sem, which):
         x, y, z, core = place()
         tp = lax.axis_index("tp")
         base = which * len(COLUMN)
+        y_lo = lax.rem(y, 2)
         self.local = pltpu.make_async_copy(
-            source.at[y * 2 + core], target.at[core, lax.rem(y, 2), x * 4 + z, tp], local_sem.at[which]
+            source.at[y * 2 + core], land(core, y_lo, tp), local_sem.at[which]
         )
         self.sent, self.got = [], []
         for n, (dy, dc) in enumerate(COLUMN):
             to_y, from_y = step(y, dy), step(y, -dy)
-            peer_core = core if dc == 0 else 1 - core
+            peer = core if dc == 0 else 1 - core
             sems = send_sems.at[base + n], recv_sems.at[base + n]
-            to = device_at(x, to_y, z, peer_core)
-            slot = target.at[peer_core, lax.rem(y, 2), x * 4 + z, tp]
-            self.sent.append(send(source.at[to_y * 2 + peer_core], slot, *sems, to))
-            ref = target.at[core, lax.rem(from_y, 2), x * 4 + z, (from_y // 2) * 2 + peer_core]
+            to = device_at(x, to_y, z, peer)
+            self.sent.append(send(source.at[to_y * 2 + peer], land(peer, y_lo, tp), *sems, to))
+            ref = land(core, lax.rem(from_y, 2), (from_y // 2) * 2 + peer)
             self.got.append(send(ref, ref, *sems, to))
 
     def start(self):
@@ -200,6 +204,11 @@
     def finish(self):
         for made in self.sent:
             made.wait_send()
+
+
+def lander(target):
+    x, _, z, _ = place()
+    return lambda core, y_lo, tp: target.at[core, y_lo, x * 4 + z, tp]
 
 
 def viewer(target, owner):
@@ -211,161 +220,316 @@
     return view
 
 
-def gather_kernel(
-    x_ref, win_ref, wout_ref, rows_ref, other_ref, gin_ref, gout_ref,
+def project_kernel(
+    tokens_ref, prompt_ref, marks_ref, win_ref, wout_ref, info_ref, gain_ref, head_gain_ref, turn_ref,
+    q_ref, pairs_ref, residual_ref, prefix_ref, meta_ref, gout_ref,
+    x_ref, rows, theirs, gin, stage, scaled, sums, squares, turn,
     a_send, a_recv, in_send, in_recv, out_send, out_recv, t_send, t_recv, p_send, p_recv, local_sem,
 ):
     x, y, z, core = place()
     tp = lax.axis_index("tp")
     y_lo, y_hi = lax.rem(y, 2), y // 2
     sibling = device_at(x, y, z, 1 - core)
+    above, below = step(y, 1), step(y, -1)
+    row_count = residual_ref.shape[0]
+    loads, at = [], 0
+    for n, ref in enumerate((tokens_ref, prompt_ref, marks_ref)):
+        loads.append(
+            pltpu.make_async_copy(ref, x_ref.at[pl.ds(at, ref.shape[0])], local_sem.at[3 + n])
+        )
+        at += ref.shape[0]
+    for load in loads:
+        load.start()
     greet(column_peers() + plane_peers())
-
-    inward_rows = Column(win_ref, gin_ref, a_send, a_recv, local_sem, 0)
-    outward_rows = Column(wout_ref, gout_ref, a_send, a_recv, local_sem, 1)
+    inward_rows = Column(
+        win_ref, lambda _, lo, at: stage.at[lo, at], a_send, a_recv, local_sem, 0
+    )
+    outward_rows = Column(wout_ref, lander(gout_ref), a_send, a_recv, local_sem, 1)
     inward_rows.start()
     outward_rows.start()
+    for load in loads:
+        load.wait()
 
     count, width = x_ref.shape
     cut = count // 32 * 16
+    parts = (pl.ds(0, cut), pl.ds(cut, count - cut))
+    home = core == y_lo
+    away = jnp.logical_not(home)
 
     def quarter(at):
         return pl.ds(pl.multiple_of(at * width, 128), width)
 
-    def token_copy(number, source, target, device):
-        return send(source, target, t_send.at[number], t_recv.at[number], device)
-
-    def pass_on(number, at, source=None):
-        ref = other_ref.at[:, quarter(at)]
-        source = rows_ref.at[:, quarter(at)] if source is None else source
-        return send(source, ref, p_send.at[number], p_recv.at[number], sibling)
-
-    home = core == y_lo
-    mine = rows_ref.at[:, quarter(tp)]
-    up = send(x_ref, mine, t_send.at[0], t_recv.at[core], device_at(x, step(y, 1), z, y_lo))
-    down = send(x_ref, mine, t_send.at[1], t_recv.at[2 + core], device_at(x, step(y, -1), z, y_lo))
-    up.start()
-    down.start()
+    def own_part(up, part):
+        to = device_at(x, above if up else below, z, y_lo)
+        at = (0 if up else 4) + core * 2 + part
+        ref = rows.at[parts[part], quarter(tp)]
+        return send(x_ref.at[parts[part]], ref, t_send.at[(0 if up else 2) + part], t_recv.at[at], to)
+
+    def token_copy(number, ref, device, source=None):
+        source = ref if source is None else source
+        return send(source, ref, t_send.at[number], t_recv.at[number], device)
+
+    def pass_on(i):
+        source = rows.at[pl.ds(0, row_count), quarter(y_hi * 2 + i)]
+        target = theirs.at[:, pl.ds(i * width, width)]
+        return send(source, target, p_send.at[i], p_recv.at[i], sibling)
+
+    mine = rows.at[:, quarter(tp)]
+    keep = pltpu.make_async_copy(x_ref, mine, local_sem.at[2])
+    own_parts = [own_part(True, 0), own_part(False, 1), own_part(True, 1), own_part(False, 0)]
+    for made in own_parts:
+        made.start()
 
     @pl.when(home)
     def _():
-        pltpu.make_async_copy(x_ref, mine, local_sem.at[2]).start()
-        pass_on(0, tp, x_ref).start()
-
-    @pl.when(jnp.logical_not(home))
+        keep.start()
+
+    @pl.when(away)
     def _():
-        token_copy(4, x_ref, mine, sibling).start()
-        pltpu.make_async_copy(x_ref, other_ref.at[:, quarter(tp)], local_sem.at[2]).start()
-
-    inward = Plane(viewer(gin_ref, core), in_send, in_recv)
+        token_copy(8, mine, sibling, x_ref).start()
+
+    def gin_viewer(owner):
+        size = stage.shape[1] * stage.shape[2]
+
+        def view(half, where, part=None):
+            start = (half * 16 + where) * size
+            if part is None:
+                return gin.at[owner, pl.ds(pl.multiple_of(start, 16), size)]
+            start = start + part * (size // 2)
+            return gin.at[owner, pl.ds(pl.multiple_of(start, 16), size // 2)]
+
+        return view
+
+    inward = Plane(gin_viewer(core), in_send, in_recv)
     outward = Plane(viewer(gout_ref, core), out_send, out_recv)
     inward_rows.ready()
+    for half in range(2):
+        block = stage[half].astype(jnp.float32)
+        inward.block(half, 0, 0)[...] = block.reshape(-1, block.shape[-1]).astype(jnp.bfloat16)
     inward.begin()
     inward.first()
     inward.opposite()
     outward_rows.ready()
     outward.begin()
-
-    def away_blocks():
-        below, above = step(y, -1), step(y, 1)
+    row_tile = 64
+    acts = list(inward.rest())
+
+    def fill_turns(tile):
+        lane = lax.broadcasted_iota(jnp.int32, (row_tile, turn.shape[3]), 1)
+        sign = jnp.where(lane < turn.shape[3] // 2, -1.0, 1.0)
+        span = slice(tile * row_tile, (tile + 1) * row_tile)
+        if tile * row_tile < row_count:
+            starts = [info_ref[span, WITHIN : WITHIN + 1] + PBLK * (n + 1) for n in range(PBLOCKS)]
+        else:
+            first = lax.broadcasted_iota(jnp.int32, (row_tile, 1), 0).astype(jnp.float32)
+            starts = [first + (tile * row_tile - row_count)]
+        for n, start in enumerate(starts):
+            angles = start * turn_ref[0:1]
+            turn[n, 0, span] = jnp.cos(angles)
+            turn[n, 1, span] = jnp.sin(angles) * sign
+
+    fill_turns(0)
+    fill_turns(1)
+    for act in acts[:3]:
+        act()
+        fill_turns(acts.index(act) + 2)
+
+    low, high = (below // 2) * 2, (above // 2) * 2
+
+    @pl.when(away)
+    def _():
         for k in range(2):
-            low = (below // 2) * 2 + k
-            high = (above // 2) * 2 + k
-            yield k, low, high, below, above
-
-    @pl.when(jnp.logical_not(home))
+            ref = rows.at[parts[0], quarter(low + k)]
+            token_copy(k * 2, ref, sibling).wait_recv()
+            token_copy(9 + k, ref, device_at(x, above, z, core)).start()
+            ref = rows.at[parts[1], quarter(high + k)]
+            token_copy(4 + k * 2 + 1, ref, sibling).wait_recv()
+            token_copy(11 + k, ref, device_at(x, below, z, core)).start()
+
+    for n, act in enumerate(acts[3:]):
+        act()
+        if n < 4:
+            fill_turns(n + 5)
+    outward.first()
+    inward.finish(gin_viewer(1 - core))
+    outward.opposite()
+    later = list(outward.rest())
+
+    def multiply(i):
+        at = quarter(y_hi * 2 + i if i < 2 else (1 - y_hi) * 2 + i - 2)
+        gain = gain_ref[:, at]
+        for tile in range(scaled.shape[0] // row_tile):
+            span = pl.ds(tile * row_tile, row_tile)
+            values = rows[span, at].astype(jnp.float32)
+            total = jnp.sum(values * values, axis=1, keepdims=True)
+            total = jnp.broadcast_to(total, (row_tile, squares.shape[1]))
+            squares[span] = total if i == 0 else squares[span] + total
+            scaled[span] = (values * gain).astype(jnp.bfloat16)
+        for half in range(2):
+            term = jnp.dot(scaled[...], gin[half, at], preferred_element_type=jnp.float32)
+            sums[half] = term if i == 0 else sums[half] + term
+
+    @pl.when(away)
     def _():
-        for k, low, high, below, above in away_blocks():
-            ref = rows_ref.at[:, quarter(low)]
-            token_copy(k, ref, ref, sibling).wait_recv()
-            ref = rows_ref.at[pl.ds(0, cut), quarter(low)]
-            token_copy(5 + k, ref, ref, device_at(x, above, z, core)).start()
-            ref = rows_ref.at[:, quarter(high)]
-            token_copy(2 + k, ref, ref, sibling).wait_recv()
-            ref = rows_ref.at[pl.ds(cut, count - cut), quarter(high)]
-            token_copy(7 + k, ref, ref, device_at(x, below, z, core)).start()
-            pass_on(k, low).start()
-            pass_on(2 + k, high).start()
-
-    inward.second_all()
-    outward.first()
-    outward.opposite()
-    outward.second_all()
-
-    @pl.when(jnp.logical_not(home))
-    def _():
-        for k, low, high, below, above in away_blocks():
-            ref = rows_ref.at[pl.ds(0, cut), quarter(low)]
-            token_copy(5 + k, ref, ref, sibling).wait_send()
-            ref = rows_ref.at[pl.ds(cut, count - cut), quarter(high)]
-            token_copy(7 + k, ref, ref, sibling).wait_send()
-            pass_on(k, low).wait_send()
-            pass_on(2 + k, high).wait_send()
-        token_copy(4, x_ref, mine, sibling).wait_send()
-        pltpu.make_async_copy(x_ref, other_ref.at[:, quarter(tp)], local_sem.at[2]).wait()
-        for number in (0, 2, 3):
-            pass_on(number, tp).wait_recv()
+        for k in range(2):
+            token_copy(k * 2 + 1, rows.at[parts[1], quarter(low + k)], sibling).wait_recv()
+            token_copy(4 + k * 2, rows.at[parts[0], quarter(high + k)], sibling).wait_recv()
+        for i in range(2):
+            pass_on(i).start()
 
     @pl.when(home)
     def _():
-        opposite = 1 - y_hi
-        for k in range(2):
-            at = quarter(opposite * 2 + k)
-            ref = rows_ref.at[pl.ds(0, cut), at]
-            token_copy(5 + k, ref, ref, sibling).wait_recv()
-            ref = rows_ref.at[pl.ds(cut, count - cut), at]
-            token_copy(7 + k, ref, ref, sibling).wait_recv()
-            pass_on(2 + k, opposite * 2 + k).start()
-        ref = rows_ref.at[:, quarter(y_hi * 2 + 1 - core)]
-        token_copy(4, ref, ref, sibling).wait_recv()
-        pltpu.make_async_copy(x_ref, mine, local_sem.at[2]).wait()
-        for number in range(4):
-            pass_on(number, tp).wait_recv()
-        pass_on(0, tp, x_ref).wait_send()
-        for k in range(2):
-            pass_on(2 + k, tp).wait_send()
-
-    up.wait_send()
-    down.wait_send()
+        keep.wait()
+        token_copy(8, rows.at[:, quarter(y_hi * 2 + 1 - core)], sibling).wait_recv()
+
+    for i in range(2):
+        multiply(i)
+    for act in later[:4]:
+        act()
+
+    @pl.when(home)
+    def _():
+        for i in range(2):
+            pass_on(i).wait_recv()
+        for i in range(2):
+            for tile in range(row_count // row_tile):
+                span = pl.ds(tile * row_tile, row_tile)
+                lanes = slice(i * width, (i + 1) * width)
+                residual_ref[span, lanes] = jnp.where(
+                    info_ref[span, CROSS : CROSS + 1] > 0.5,
+                    theirs[span, lanes].astype(jnp.float32),
+                    rows[span, quarter(y_hi * 2 + i)].astype(jnp.float32),
+                ).astype(jnp.bfloat16)
+
+    for k in range(2):
+
+        @pl.when(home)
+        def _():
+            at = (1 - y_hi) * 2 + k
+            for part in range(2):
+                token_copy(9 + 2 * part + k, rows.at[parts[part], quarter(at)], sibling).wait_recv()
+
+        multiply(2 + k)
+
+    meta_ref[...] = rows[count - META : count, 0:128]
+    meta = meta_ref[...].astype(jnp.float32)[0:1]
+    half_heads = q_ref.shape[0] // 2
+    slots = 4.0
+    head = q_ref.shape[2]
+    for tile in range(scaled.shape[0] // row_tile):
+        span = slice(tile * row_tile, (tile + 1) * row_tile)
+        scale = lax.rsqrt(squares[span] * (1.0 / (4 * width)) + epsilon)
+        if tile * row_tile < row_count:
+            lane = lax.broadcasted_iota(jnp.int32, (row_tile, 128), 1).astype(jnp.float32)
+            blocks = jnp.sum(
+                jnp.where(lane == info_ref[span, SLOT : SLOT + 1] + slots, meta, 0.0),
+                axis=1, keepdims=True,
+            )
+            prefix_ref[span] = jnp.broadcast_to(blocks * PBLK, (row_tile, 128))
+            two = jnp.broadcast_to(blocks, (row_tile, head)) > 1.5
+            turns = [jnp.where(two, turn[1, n, span], turn[0, n, span]) for n in range(2)]
+        else:
+            turns = [turn[0, n, span] for n in range(2)]
+
+        def turned(values, gain):
+            values = values * scale
+            values = values * lax.rsqrt(jnp.mean(values * values, axis=1, keepdims=True) + epsilon)
+            values = values * gain
+            swapped = jnp.concatenate([values[:, head // 2 :], values[:, : head // 2]], axis=1)
+            return (values * turns[0] + swapped * turns[1]).astype(jnp.bfloat16)
+
+        if tile * row_tile < row_count:
+            for h in range(2 * half_heads):
+                column = h % half_heads * head
+                q_ref[h, span] = turned(
+                    sums[h // half_heads, span, column : column + head], head_gain_ref[0:1]
+                )
+        column = half_heads * head
+        pairs_ref[span, :head] = turned(sums[0, span, column : column + head], head_gain_ref[1:2])
+        pairs_ref[span, head:] = (sums[1, span, column : column + head] * scale).astype(jnp.bfloat16)
+
+    for act in later[4:]:
+        act()
+    outward.finish(viewer(gout_ref, 1 - core))
     inward_rows.finish()
     outward_rows.finish()
-    inward.finish(viewer(gin_ref, 1 - core))
-    outward.finish(viewer(gout_ref, 1 - core))
-
-
-def gather_all(rows, win, wout):
-    count, width = rows.shape
-    sems = [14, 14, Plane.COPIES, Plane.COPIES, Plane.COPIES, Plane.COPIES, 9, 9, 4, 4, 3]
+    for made in own_parts:
+        made.wait_send()
+
+    @pl.when(away)
+    def _():
+        for k in range(2):
+            token_copy(9 + k, rows.at[parts[0], quarter(low + k)], sibling).wait_send()
+            token_copy(11 + k, rows.at[parts[1], quarter(high + k)], sibling).wait_send()
+            pass_on(k).wait_send()
+        token_copy(8, mine, sibling, x_ref).wait_send()
+
+
+def project(tokens, prompts, marks, win, wout, head, *tables):
+    row_count, width = tokens.shape
+    used = row_count + prompts.shape[0]
+    count = used + META
+    heads = 2 * (win.shape[2] // head - 1)
+    bf16 = jnp.bfloat16
+    planes = [Plane.COPIES] * 4
     return pl.pallas_call(
-        gather_kernel,
-        name="gather_all",
+        project_kernel,
+        name="project",
         out_shape=(
-            jax.ShapeDtypeStruct((count, 4 * width), rows.dtype),
-            jax.ShapeDtypeStruct((count, 4 * width), rows.dtype),
-            jax.ShapeDtypeStruct((2, 2, 16, 4) + win.shape[1:], win.dtype),
-            jax.ShapeDtypeStruct((2, 2, 16, 4) + wout.shape[1:], wout.dtype),
+            jax.ShapeDtypeStruct((heads, row_count, head), bf16),
+            jax.ShapeDtypeStruct((used, 2 * head), bf16),
+            jax.ShapeDtypeStruct((row_count, 2 * width), bf16),
+            jax.ShapeDtypeStruct((row_count, 128), jnp.float32),
+            jax.ShapeDtypeStruct((META, 128), bf16),
+            jax.ShapeDtypeStruct((2, 2, 16, 4) + wout.shape[1:], bf16),
         ),
-        in_specs=[ANY] * 3,
-        out_specs=(ANY,) * 4,
-        scratch_shapes=[pltpu.SemaphoreType.DMA((n,)) for n in sems],
-        compiler_params=pltpu.CompilerParams(collective_id=0, has_side_effects=True),
-    )(rows, win, wout)
+        in_specs=[ANY] * 5 + [VMEM] * len(tables),
+        out_specs=(VMEM,) * 5 + (ANY,),
+        scratch_shapes=[
+            pltpu.VMEM((count, width), bf16),
+            pltpu.VMEM((count, 4 * width), bf16),
+            pltpu.VMEM((row_count, 2 * width), bf16),
+            pltpu.VMEM((2, 4 * width, win.shape[2]), bf16),
+            pltpu.VMEM((2, 4) + win.shape[1:], bf16),
+            pltpu.VMEM((used, width), bf16),
+            pltpu.VMEM((2, used, win.shape[2]), jnp.float32),
+            pltpu.VMEM((used, 128), jnp.float32),
+            pltpu.VMEM((PBLOCKS, 2, used, head), jnp.float32),
+        ]
+        + [pltpu.SemaphoreType.DMA((n,)) for n in [14, 14] + planes + [13, 13, 2, 2, 6]],
+        compiler_params=pltpu.CompilerParams(
+            collective_id=0, has_side_effects=True, vmem_limit_bytes=58 * 2**20
+        ),
+    )(tokens, prompts, marks, win, wout, *tables)
 
 
 TILE = 64
 
 
 def attend_kernel(
-    q_ref, own_ref, prompt_ref, bounds_ref, group_ref, wout_ref, out_ref, gout_ref,
-    prompts, shared, total, sums, a_send, a_recv, out_send, out_recv, kv_send, kv_recv, local_sem,
+    q_hbm, pairs_hbm, info_hbm, prefix_hbm, group_ref, wout_ref, out_ref, gout_ref,
+    q_ref, pairs_ref, bounds_ref, prefix_ref, mine_ref, theirs_ref,
+    prompts, shared, total, sums, x_send, x_recv, load_sem, a_send, a_recv, out_send, out_recv, kv_send, kv_recv, local_sem,
 ):
     x, y, z, core = place()
-    head = prompt_ref.shape[1] // 2
-    heads = q_ref.shape[0]
+    heads, row_count, head = q_ref.shape
+    loads = [
+        pltpu.make_async_copy(hbm, ref, load_sem.at[n])
+        for n, (hbm, ref) in enumerate(
+            ((pairs_hbm, pairs_ref), (q_hbm, q_ref), (info_hbm, bounds_ref), (prefix_hbm, prefix_ref))
+        )
+    ]
+    for load in loads:
+        load.start()
+    own_ref = pairs_ref.at[pl.ds(0, row_count)]
+    prompt_ref = pairs_ref.at[pl.ds(row_count, prompts.shape[1])]
+    sibling = device_at(x, y, z, 1 - core)
     greet(column_peers() + plane_peers())
+    for load in loads:
+        load.wait()
     mine = pltpu.make_async_copy(prompt_ref, prompts.at[core * 16 + x * 4 + z], local_sem.at[1])
     mine.start()
-    rows = Column(wout_ref, gout_ref, a_send, a_recv, local_sem, 0)
+    rows = Column(wout_ref, lander(gout_ref), a_send, a_recv, local_sem, 0)
     rows.start()
     mine.wait()
 
@@ -388,7 +552,7 @@
             queries, keys, (((1,), (1,)), ((), ())), preferred_element_type=jnp.float32
         )
         count = keys.shape[0]
-        at = lax.broadcasted_iota(jnp.int32, (TILE, count), 1)
+        at = lax.broadcasted_iota(jnp.int32, (TILE, count), 1).astype(jnp.float32)
         allowed = (at >= low) & (at < high)
         weights = jnp.where(
             allowed[None], jnp.exp2(scores.reshape(heads, TILE, count) * scale), 0.0
@@ -401,20 +565,28 @@
 
     def own_tile(tile):
         span = slice(tile * TILE, (tile + 1) * TILE)
-        count = min(-(-(tile + 1) * TILE // 128) * 128, own_ref.shape[0])
-        low = bounds_ref[span, 0:1]
-        high = lax.broadcasted_iota(jnp.int32, (TILE, 1), 0) + (tile * TILE + 1)
+        count = min(-(-(tile + 1) * TILE // 128) * 128, row_count)
+        low = bounds_ref[span, START : START + 1]
+        high = lax.broadcasted_iota(jnp.int32, (TILE, 1), 0).astype(jnp.float32) + (tile * TILE + 1.0)
         span, weight, blend = weigh(tile, own_ref[:count, :head], own_ref[:count, head:], low, high)
         total[:, span] = blend
         sums[:, span] = jnp.broadcast_to(weight, (heads, TILE, head))
 
     def shared_tile(tile):
         span = slice(tile * TILE, (tile + 1) * TILE)
-        low, high = bounds_ref[span, 1:2], bounds_ref[span, 2:3]
+        low = bounds_ref[span, PROMPT : PROMPT + 1]
+        high = low + prefix_ref[span, 0:1]
         span, weight, blend = weigh(tile, shared[:, :head], shared[:, head:], low, high)
         blend = (total[:, span] + blend) / (sums[:, span] + weight)
         for h in range(heads):
-            out_ref[span, h * head : (h + 1) * head] = blend[h].astype(jnp.bfloat16)
+            mine_ref[span, h * head : (h + 1) * head] = blend[h].astype(jnp.bfloat16)
+        swap(tile).start()
+
+    def swap(tile):
+        span = pl.ds(tile * TILE, TILE)
+        return send(
+            mine_ref.at[span], theirs_ref.at[span], x_send.at[tile], x_recv.at[tile], sibling
+        )
 
     tiles = q_ref.shape[1] // TILE
     for tile in range(4):
@@ -443,13 +615,24 @@
         shared_tile(tile)
     for act in later[tiles:]:
         act()
+    for tile in range(tiles):
+        swap(tile).wait_recv()
+        span = slice(tile * TILE, (tile + 1) * TILE)
+        out_ref[span] = jnp.where(
+            bounds_ref[span, CROSS : CROSS + 1] > 0.5,
+            theirs_ref[span].astype(jnp.float32),
+            mine_ref[span].astype(jnp.float32),
+        ).astype(jnp.bfloat16)
+        swap(tile).wait_send()
     rows.finish()
     outward.finish(viewer(gout_ref, 1 - core))
 
 
-def attend(queries, own, prompt, bounds, group, wout):
+def attend(queries, pairs, info, prefix, group, wout):
     heads, count, head = queries.shape
-    sems = [7, 7, Plane.COPIES, Plane.COPIES, Plane.COPIES, Plane.COPIES, 2]
+    prompt = (pairs.shape[0] - count, pairs.shape[1])
+    tiles = count // TILE
+    sems = [tiles, tiles, 4, 7, 7] + [Plane.COPIES] * 4 + [2]
     return pl.pallas_call(
         attend_kernel,
         name="attend",
@@ -457,11 +640,17 @@
             jax.ShapeDtypeStruct((count, heads * head), jnp.bfloat16),
             jax.ShapeDtypeStruct((2, 2, 16, 4) + wout.shape[1:], wout.dtype),
         ),
-        in_specs=[VMEM] * 4 + [pl.BlockSpec(memory_space=pltpu.SMEM), ANY],
+        in_specs=[ANY] * 4 + [pl.BlockSpec(memory_space=pltpu.SMEM), ANY],
         out_specs=(VMEM, ANY),
         scratch_shapes=[
-            pltpu.VMEM((32,) + prompt.shape, prompt.dtype),
-            pltpu.VMEM((group.shape[0] * prompt.shape[0], prompt.shape[1]), prompt.dtype),
+            pltpu.VMEM(queries.shape, queries.dtype),
+            pltpu.VMEM(pairs.shape, pairs.dtype),
+            pltpu.VMEM(info.shape, info.dtype),
+            pltpu.VMEM(prefix.shape, prefix.dtype),
+            pltpu.VMEM((count, heads * head), jnp.bfloat16),
+            pltpu.VMEM((count, heads * head), jnp.bfloat16),
+            pltpu.VMEM((32,) + prompt, pairs.dtype),
+            pltpu.VMEM((group.shape[0] * prompt[0], prompt[1]), pairs.dtype),
             pltpu.VMEM(queries.shape, jnp.float32),
             pltpu.VMEM(queries.shape, jnp.float32),
         ]
@@ -469,7 +658,7 @@
         compiler_params=pltpu.CompilerParams(
             collective_id=1, has_side_effects=True, vmem_limit_bytes=48 * 2**20
         ),
-    )(queries, own, prompt, bounds, group, wout)
+    )(queries, pairs, info, prefix, group, wout)
 
 
 BLOCK = 128
@@ -500,14 +689,45 @@
             end_z = (z + (2 * far_z.astype(jnp.int32) if level in ("z1", "x1") else 0)) % 4
             odd_x, far_x = level_bits(along_z(shift, end_z)[1] % 4, sign)
             masks.append({"z1": odd_z, "x1": odd_x, "z2": far_z, "x2": far_x}[level])
-    masks = jnp.stack(masks).astype(jnp.float32)
-    return jnp.broadcast_to(masks[:, :, None], masks.shape + (BLOCK,))
+    return [mask.astype(jnp.float32) for mask in masks]
+
+
+def return_order(blocks):
+    unit, seen, ahead, pace = 1.28, 1.6, 3.0, 8.2
+    cost = {"multiply": 1.6, "add": 0.5, "finish": 0.4, "take": 0.3}
+    free, summed, order, now = {}, {}, [], 0.0
+    waiting = [(max(0.0, pace * p - ahead), 0, ("multiply", p)) for p in range(blocks // 2)]
+
+    def use(link, long):
+        free[link] = max(free.get(link, 0.0), now) + long
+        return free[link]
+
+    while waiting:
+        ready, _, act = waiting.pop(waiting.index(min(waiting)))
+        now = max(now, ready) + cost[act[0]]
+        order.append(act)
+        if act[0] == "multiply":
+            both = (2 * act[1], 2 * act[1] + 1)
+            for j in both:
+                waiting.append((use("y", unit) + seen, 1, ("add", j)))
+            for j in both:
+                summed[j] = use("y", unit)
+        elif act[0] == "add":
+            waiting.append((max(use("y", unit), summed[act[1]]) + seen, 2, ("finish", act[1])))
+        else:
+            j, level = act[1], 0 if act[0] == "finish" else act[2] + 1
+            if level < len(LEVELS):
+                axis, far = LEVELS[level][0], LEVELS[level][1] == "2"
+                links = (axis + "+", axis + "-") if far else (axis + "+-"[j % 2],)
+                end = max([use(link, 2 * unit) for link in links]) + (0.5 if far else 0.0)
+                waiting.append((end + seen, 3 + level, ("take", j, level)))
+    return order
 
 
 def return_kernel(
-    blend_ref, w0_ref, w1_ref, residual_ref, mask_ref, out_ref,
-    sums, source, home_sum, home_got, raw, final, held, landed,
-    src_send, raw_recv, fin_recv, move_send, move_recv,
+    blend_hbm, w0_hbm, w1_hbm, residual_hbm, info_ref, out_ref,
+    blend_ref, residual_ref, w0_ref, w1_ref, mask_ref, sums, source, home_sum, home_got, raw, final, held, landed,
+    src_send, raw_recv, fin_recv, move_send, move_recv, w_sem,
 ):
     x, y, z, core = place()
     y_lo, y_hi = lax.rem(y, 2), y // 2
@@ -515,6 +735,19 @@
     blocks = width // BLOCK
     above, below = step(y, 1), step(y, -1)
     sibling = device_at(x, y, z, 1 - core)
+    loads = [
+        pltpu.make_async_copy(hbm.at[half], ref.at[half], w_sem.at[n * 2 + half])
+        for n, (hbm, ref) in enumerate(((w0_hbm, w0_ref), (w1_hbm, w1_ref)))
+        for half in range(2)
+    ]
+    loads.append(pltpu.make_async_copy(blend_hbm, blend_ref, w_sem.at[4]))
+    loads.append(pltpu.make_async_copy(residual_hbm, residual_ref, w_sem.at[5]))
+    for load in loads:
+        load.start()
+    for n in range(mask_ref.shape[0]):
+        mask_ref[n] = jnp.broadcast_to(
+            info_ref[:, MOVES + n : MOVES + n + 1], mask_ref.shape[1:]
+        )
     peers = [device_at(x, at, z, k) for at in (above, below) for k in range(2)] + [sibling]
     peers += [device_at(step(x, s), y, z, core) for s in (1, -1, 2)]
     peers += [device_at(x, y, step(z, s), core) for s in (1, -1, 2)]
@@ -530,7 +763,10 @@
         jnp.where(home, y_hi * 2 + core, down * 2),
     )
     pieces = w0_ref.shape[0]
-    depth = w0_ref.shape[2]
+    half_depth = w0_ref.shape[2] + w1_ref.shape[2]
+
+    for load in loads:
+        load.wait()
 
     def raw_copy(j, slot):
         to = device_at(x, (above, below)[slot], z, core)
@@ -555,7 +791,8 @@
             total = None
             for half in range(pieces):
                 for n, w_ref in enumerate((w0_ref, w1_ref)):
-                    column = (half * 2 + n) * depth
+                    column = half * half_depth + n * w0_ref.shape[2]
+                    depth = w_ref.shape[2]
                     term = lax.dot_general(
                         blend_ref[:, column : column + depth], w_ref[half, pl.ds(start, 2 * BLOCK)],
                         (((1,), (1,)), ((), ())), preferred_element_type=jnp.float32,
@@ -639,19 +876,8 @@
         else:
             out_ref[:, j * BLOCK : (j + 1) * BLOCK] = chosen
 
-    for tick in range(blocks + 2 + len(LEVELS)):
-        if tick < blocks // 2:
-            multiply(tick)
-        for j in range(blocks):
-            if tick == j + 1:
-                add(j)
-        for j in range(blocks):
-            if tick == j + 2:
-                finish(j)
-        for level in reversed(range(len(LEVELS))):
-            j = tick - 3 - level
-            if 0 <= j < blocks:
-                take(j, level)
+    for act, *which in return_order(blocks):
+        {"multiply": multiply, "add": add, "finish": finish, "take": take}[act](*which)
 
     for j in range(blocks):
         for level in range(len(LEVELS)):
@@ -669,7 +895,7 @@
                 final_copy(j, at).wait_send()
 
 
-def return_rows(blended, w0, w1, residual, masks):
+def return_rows(blended, w0, w1, residual, info):
     count = blended.shape[0]
     width = residual.shape[1] // 2
     blocks = width // BLOCK
@@ -682,9 +908,14 @@
         return_kernel,
         name="return_rows",
         out_shape=jax.ShapeDtypeStruct((count, width), jnp.bfloat16),
-        in_specs=[VMEM] * 5,
+        in_specs=[ANY] * 4 + [VMEM],
         out_specs=VMEM,
         scratch_shapes=[
+            pltpu.VMEM(blended.shape, blended.dtype),
+            pltpu.VMEM(residual.shape, residual.dtype),
+            pltpu.VMEM(w0.shape, w0.dtype),
+            pltpu.VMEM(w1.shape, w1.dtype),
+            pltpu.VMEM((2 * levels, count, BLOCK), jnp.float32),
             pltpu.VMEM((4, count, 2 * BLOCK), jnp.float32),
             room(4),
             pltpu.VMEM((blocks, count, BLOCK), jnp.float32),
@@ -694,32 +925,12 @@
             room(levels),
             room(levels),
         ]
-        + [pltpu.SemaphoreType.DMA((n * blocks,)) for n in (4, 2, 3, levels, levels)],
+        + [pltpu.SemaphoreType.DMA((n * blocks,)) for n in (4, 2, 3, levels, levels)]
+        + [pltpu.SemaphoreType.DMA((6,))],
         compiler_params=pltpu.CompilerParams(
             collective_id=2, has_side_effects=True, vmem_limit_bytes=56 * 2**20
         ),
-    )(blended, w0, w1, residual, masks)
-
-
-def rms_rows(values, gain_row):
-    floats = values.astype(jnp.float32)
-    scaled = lax.rsqrt(jnp.mean(floats * floats, axis=-1, keepdims=True) + epsilon)
-    return floats * scaled * gain_row
-
-
-def rotary(values, positions):
-    half_size = values.shape[-1] // 2
-    spread = jnp.arange(half_size, dtype=jnp.float32) * (2.0 / values.shape[-1])
-    frequency = rope_base ** (-spread)
-    angles = positions.astype(jnp.float32)[:, None] * frequency[None, :]
-    cosine = jnp.cos(angles)[:, None, :]
-    sine_part = jnp.sin(angles)[:, None, :]
-    front_half = values[..., :half_size]
-    back_half = values[..., half_size:]
-    return jnp.concatenate(
-        [front_half * cosine - back_half * sine_part, back_half * cosine + front_half * sine_part],
-        axis=-1,
-    )
+    )(blended, w0, w1, residual, info)
 
 
 def slot_layout(seq_lengths, row_count):
@@ -762,55 +973,41 @@
     value_cols = w_value.astype(jnp.bfloat16).reshape(depth, groups, 1, head_size)
     win = jnp.concatenate([halves, jnp.concatenate([key_cols, value_cols], axis=2)], axis=3)
     win = win.transpose(1, 2, 0, 3).reshape(2 * groups, depth, -1)
-    wout = w_out.astype(jnp.bfloat16).reshape(2 * groups, 2, -1, depth).transpose(1, 0, 3, 2)
-    meta = jnp.concatenate([prompt_group, prompt_blocks]).astype(jnp.bfloat16)
-    meta = jnp.pad(meta[None, :], ((0, META - 1), (0, width - 2 * slot_count)))
-    rows, other, gin, gout = gather_all(
-        jnp.concatenate([tokens, prompt_rows, meta], axis=0), win, wout[0]
-    )
+    wout = w_out.astype(jnp.bfloat16).reshape(2 * groups, -1, depth)
+    wout = [part.transpose(0, 2, 1) for part in (wout[:, :EARLY], wout[:, EARLY:])]
+    marks = jnp.concatenate([prompt_group, prompt_blocks]).astype(jnp.bfloat16)
+    marks = jnp.pad(marks[None, :], ((0, META - 1), (0, width - 2 * slot_count)))
 
     plane_x, plane_z = rep // 4 % 4, rep % 4
     slot_of, within, onehot = slot_layout(seq_lengths, row_count)
     crosses = y_shift(dest_offset, plane_x, plane_z)
-    pair = jnp.stack([rows[row_count + prompt_len], other[row_count + prompt_len]])
-    pair = pair[:, : 2 * slot_count].astype(jnp.int32).reshape(2, 2, slot_count)
-    group_here, blocks_here = jnp.where(crosses, pair[1], pair[0])
     shift_rows = jnp.sum(onehot * dest_offset[None, :], axis=1)
-    row_crosses = jnp.sum(onehot * crosses[None, :], axis=1) == 1
-    inputs = jnp.where(row_crosses[:, None], other[:row_count], rows[:row_count])
-    normed = rms_rows(
-        jnp.concatenate([inputs, rows[row_count : row_count + prompt_len]], axis=0), norm_gain
-    ).astype(jnp.bfloat16)
-    features = normed.shape[1]
-    gin = gin.reshape(2, features, -1)
-    left = jnp.dot(normed, gin[0], preferred_element_type=jnp.float32)
-    right = jnp.dot(normed, gin[1], preferred_element_type=jnp.float32)
-    half_width = left.shape[1] - head_size
-    query_sum = jnp.concatenate([left[:row_count, :half_width], right[:row_count, :half_width]], axis=1)
-    key_sum, values_all = left[:, half_width:], right[:, half_width:].astype(jnp.bfloat16)
-    q_heads = query_sum.shape[1] // head_size
-
-    prefix_len = jnp.sum(onehot * (blocks_here * PBLK)[None, :], axis=1)
-    positions = prefix_len + within
-    queries = rotary(rms_rows(query_sum.reshape(row_count, q_heads, head_size), q_gain), positions)
-    queries = queries.astype(jnp.bfloat16).transpose(1, 0, 2)
-    all_positions = jnp.concatenate([positions, jnp.arange(prompt_len, dtype=jnp.int32)])
-    keys_all = rotary(rms_rows(key_sum[:, None], k_gain), all_positions).astype(jnp.bfloat16)[:, 0]
-    pairs = jnp.concatenate([keys_all, values_all], axis=1)
-    bounds = jnp.stack(
-        [jnp.arange(row_count, dtype=jnp.int32) - within, slot_of * prompt_len, slot_of * prompt_len + prefix_len], axis=1
+    row_crosses = jnp.sum(onehot * crosses[None, :], axis=1)
+    lanes = {
+        CROSS: row_crosses,
+        START: jnp.arange(row_count, dtype=jnp.int32) - within,
+        PROMPT: slot_of * prompt_len,
+        SLOT: slot_of,
+        WITHIN: within,
+    }
+    for n, mask in enumerate(move_masks(shift_rows, plane_x, plane_z)):
+        lanes[MOVES + n] = mask
+    lane = jnp.arange(128, dtype=jnp.int32)[None, :]
+    info = jnp.zeros((row_count, 128), jnp.float32)
+    for at, values in lanes.items():
+        info = jnp.where(lane == at, values.astype(jnp.float32)[:, None], info)
+    spread = np.arange(head_size // 2, dtype=np.float32) * np.float32(2.0 / head_size)
+    frequency = np.float32(rope_base) ** -spread
+    frequency = jnp.asarray(np.tile(frequency.astype(np.float32), 2)[None, :])
+    queries, pairs, residual, prefix, meta, gout = project(
+        tokens, prompt_rows, marks, win, wout[0], head_size,
+        info, norm_gain[None, :], jnp.stack([q_gain, k_gain]), frequency,
     )
-    bounds = jnp.pad(bounds, ((0, 0), (0, head_size - 3)))
-    blended, gout_b = attend(
-        queries, pairs[:row_count], pairs[row_count:], bounds, group_here, wout[1]
-    )
-    gout, gout_b = gout.reshape(2, features, -1), gout_b.reshape(2, features, -1)
-    residual = lax.dynamic_slice_in_dim(
-        inputs, lax.axis_index("tp") // 2 * (2 * width), 2 * width, axis=1
-    )
+    group_here = meta[0, :slot_count].astype(jnp.int32)
+    blended, gout_b = attend(queries, pairs, info, prefix, group_here, wout[1])
+    features = 4 * width
     return return_rows(
-        blended, gout, gout_b, residual,
-        move_masks(shift_rows, plane_x, plane_z),
+        blended, gout.reshape(2, features, -1), gout_b.reshape(2, features, -1), residual, info
     )
 
 

time: 270 us -> 237 us (0.88)
  local copies, waits for them, and re-layouts: 20.6 us -> 7.55 us
  matrix products: 9.72 us -> 0 us
  other arithmetic: 17.8 us -> 11.8 us
  Pallas kernels: 219 us -> 214 us
    pallas_call x1, Pallas kernels: 102 us -> 85.5 us  [return_rows(): pl.pallas_call(return_kernel, name='return_rows', out_shape=jax.ShapeDtyp...]
    slice x9 -> x2, local copies, waits for them, and re-layouts: 10.1 us -> 0.04 us  [the longest x1 0.03 us: shards(): wout[:, EARLY:]]
    dot_general x2 -> x0, matrix products: 9.72 us -> none  [the longest x1 4.89 us: shards(): right = jnp.dot(normed, gin[1], preferred_element_type=jnp.float32)]
    pallas_call x1, Pallas kernels: 75.7 us -> 81.5 us  [project(): pl.pallas_call(project_kernel, name='project', out_shape=(jax.ShapeDtypeS...]
    pallas_call x1, Pallas kernels: 41.4 us -> 47.1 us  [attend(): pl.pallas_call(attend_kernel, name='attend', out_shape=(jax.ShapeDtypeStr...]
    concatenate x5 -> x2, other arithmetic: 5.03 us -> 1.37 us  [shards(): marks = jnp.concatenate([prompt_group, prompt_blocks]).astype(jnp.bfloat16)]
    unnamed x22 -> x16, local copies, waits for them, and re-layouts: 3.7 us -> 7.12 us
    dynamic_slice x1 -> x0, local copies, waits for them, and re-layouts: 3.21 us -> none  [shards(): lax.dynamic_slice_in_dim(inputs, lax.axis_index('tp') // 2 * (2 * width),...]
where the time goes in v3:
time: 237 us; the launch traced here: 234 us
  Pallas kernels  214 us (90%)
  other arithmetic  11.8 us (5%)
  local copies, waits for them, and re-layouts  7.55 us (3%)
    pallas_call x1, Pallas kernels, return_rows(): pl.pallas_call(return_kernel, name='return_rows', out_shape=jax.ShapeDtyp...  85.5 us
    pallas_call x1, Pallas kernels, project(): pl.pallas_call(project_kernel, name='project', out_shape=(jax.ShapeDtypeS...  81.5 us
    pallas_call x1, Pallas kernels, attend(): pl.pallas_call(attend_kernel, name='attend', out_shape=(jax.ShapeDtypeStr...  47.1 us
    unnamed x16, local copies, waits for them, and re-layouts  7.12 us

profile of v3, /device:TPU:16, one launch (start us, length us, event | category | flops | bytes accessed | tf_op | source)
XLA Modules:
  0.0 233.6 jit_solution(7065872295282380763)
XLA Ops:
  0.0 0.0 copy-start.5
  0.0 0.8 compare_convert_fusion
  0.8 0.8 reduce-window.8
  1.6 0.7 bitcast_subtract_fusion
  2.2 1.3 pad_maximum_fusion.head_gain_ref
  3.5 0.7 convert_bitcast_fusion
  4.2 0.1 convert_reduce_fusion
  4.3 0.8 select_reduce_fusion.2
  5.2 0.7 fusion.5.marks_ref
  5.9 0.9 convert_element_type.154
  6.8 0.9 convert_element_type.155
  7.7 1.5 select_select_fusion.info_ref.info_hbm
  9.3 1.1 convert_element_type.153
  10.4 0.2 reshape.332
  10.6 0.1 copy.25
  10.7 0.8 maximum_maximum_fusion
  11.5 0.0 copy-done.5
  11.6 0.0 copy-start
  11.6 0.1 copy.30
  11.8 0.6 copy.34
  12.4 81.5 %project.1 = (bf16[8,448,128]{2,1,0:T(8,128)(2,1)}, bf16[576,256]{1,0:T(8,128)(2,1)}, bf16[448,2560]{1,0:T(8,128)(2,1)}, f32[448,128]{1,0:T(8,128)}, bf16[16,128...) custom-call(bf16[448,1280]{1,0:T(8,128)(2,1)} %tokens_ref.1, bf16[128,1280]{1,0:T(8,128)(2,1)} %prompt_ref.1, ...), custom_call_target="tpu_custom_call" | custom-call | tf_op jit(solution)/shard_map/project/pallas_call | solution.py:475
  93.9 0.7 bitcast_convert_fusion.group_ref
  94.6 0.0 copy-done
  94.6 0.0 copy-start.1
  94.6 1.2 copy-done.1
  95.8 0.0 copy-start.3
  95.8 1.0 copy-done.3
  96.7 0.0 copy-start.4
  96.7 0.9 copy-done.4
  97.7 47.1 %attend.1 = (bf16[448,1024]{1,0:T(8,128)(2,1)S(1)}, bf16[2,2,16,4,40,384]{5,4,3,2,1,0:T(8,128)(2,1)}) custom-call(bf16[8,448,128]{2,1,0:T(8,128)(2,1)S(1)} %copy-done.1, bf16[576,256]{1,0:T(8,128)(2,1)S(1)} %copy-done.3, f32[448,128]{1,0:T(8,128)S(1)} %copy-done, f32[448,128]{1,0:T(8,128)S(1)} %copy-done.4, s32[4]{0:T(128)S(1)} %bitcast_convert_fusion.group_ref, ...), custom_call_target="tpu_custom_call" | custom-call | tf_op jit(solution)/shard_map/attend/pallas_call | solution.py:636
  144.8 0.0 copy-start.2
  144.8 0.9 copy-done.2
  145.8 85.5 %return_rows.1 = bf16[448,1280]{1,0:T(8,128)(2,1)} custom-call(bf16[448,1024]{1,0:T(8,128)(2,1)} %copy-done.2, bf16[2,5120,128]{2,1,0:T(8,128)(2,1)} %bitcast.30, bf16[2,5120,384]{2,1,0:T(8,128)(2,1)} %bitcast.29, bf16[448,2560]{1,0:T(8,128)(2,1)} %get-tuple-element.20.residual_hbm, f32[448,128]{1,0:T(8,128)} %select_select_fusion.info_ref.info_hbm), custom_call_target="tpu_custom_call" | custom-call | tf_op jit(solution)/shard_map/return_rows/pallas_call | solution.py:907
  231.3 2.3 copy.36
  (19 shorter events, 0.3 us)
Async XLA Ops:
  0.0 11.5 %copy-start.5 = (f32[4096,40]{0,1:T(8,128)S(1)}, f32[4096,40]{0,1:T(8,128)}, u32[]{:S(2)}) copy-start(f32[4096,40]{0,1:T(8,128)} %param.20) | copy-start | bytes 1966084
  11.6 83.0 %copy-start = (f32[448,128]{1,0:T(8,128)S(1)}, f32[448,128]{1,0:T(8,128)}, u32[]{:S(2)}) copy-start(f32[448,128]{1,0:T(8,128)} %select_select_fusion.info_ref.info_hbm) | copy-start | bytes 688132
  94.6 1.2 copy-start.1
  95.8 1.0 copy-start.3
  96.7 0.9 copy-start.4
  144.8 0.9 copy-start.2

commit v4 on v3

--- a/solution.py
+++ b/solution.py
@@ -13,10 +13,11 @@
 MESH = pl.DeviceIdType.MESH
 ANY = pl.BlockSpec(memory_space=pl.ANY)
 VMEM = pl.BlockSpec(memory_space=pltpu.VMEM)
+SMEM = pl.BlockSpec(memory_space=pltpu.SMEM)
 OFFSETS = (0, -1, 1, 2)
 META = 16
 CROSS, START, PROMPT, SLOT, WITHIN, MOVES = 0, 1, 2, 3, 4, 8
-EARLY = 128
+EARLY = 256
 
 epsilon = 1e-06
 rope_base = 1000000.0
@@ -220,10 +221,73 @@
     return view
 
 
+BLOCK = 128
+LEVELS = ("z1", "x1", "z2", "x2")
+
+
+def count_of(condition):
+    return jnp.where(condition, 1, 0)
+
+
+def level_bits(shift, sign):
+    odd = (shift & 1) == 1
+    far = (shift >= 2) if sign == 1 else ((shift == 1) | (shift == 2))
+    return odd, far
+
+
+def along_z(shift, z):
+    return (shift >> 2) + count_of(z < (shift & 3))
+
+
+def y_shift(shift, x, z):
+    need_x = along_z(shift, (z + shift) & 3)
+    end_x = (x + need_x) & 3
+    return (((need_x >> 2) + count_of(end_x < (need_x & 3))) & 1) == 1
+
+
+def move_masks(shift, x, z):
+    masks = []
+    for sign in (1, -1):
+        odd_z, far_z = level_bits(shift & 3, sign)
+        for level in LEVELS:
+            end_z = (z + 2 * count_of(far_z)) & 3 if level in ("z1", "x1") else z
+            odd_x, far_x = level_bits(along_z(shift, end_z) & 3, sign)
+            masks.append({"z1": odd_z, "x1": odd_x, "z2": far_z, "x2": far_x}[level])
+    return masks
+
+
+def row_info(first, rows, lengths_ref, offsets_ref, prompt_len, x, z):
+    shape = (rows, 128)
+    row = lax.broadcasted_iota(jnp.int32, shape, 0) + first
+    lane = lax.broadcasted_iota(jnp.int32, shape, 1)
+    slot, start = jnp.zeros(shape, jnp.int32), jnp.zeros(shape, jnp.int32)
+    shift, end = jnp.zeros(shape, jnp.int32) + offsets_ref[0], 0
+    for j in range(1, lengths_ref.shape[0]):
+        end = end + lengths_ref[j - 1]
+        past = row >= end
+        slot = slot + count_of(past)
+        start = jnp.where(past, end, start)
+        shift = jnp.where(past, offsets_ref[j], shift)
+    lanes = {
+        CROSS: count_of(y_shift(shift, x, z)),
+        START: start,
+        PROMPT: slot * prompt_len,
+        SLOT: slot,
+        WITHIN: row - start,
+    }
+    for n, mask in enumerate(move_masks(shift, x, z)):
+        lanes[MOVES + n] = count_of(mask)
+    info = jnp.zeros(shape, jnp.int32)
+    for at, values in lanes.items():
+        info = jnp.where(lane == at, values, info)
+    return info.astype(jnp.float32)
+
+
 def project_kernel(
-    tokens_ref, prompt_ref, marks_ref, win_ref, wout_ref, info_ref, gain_ref, head_gain_ref, turn_ref,
-    q_ref, pairs_ref, residual_ref, prefix_ref, meta_ref, gout_ref,
-    x_ref, rows, theirs, gin, stage, scaled, sums, squares, turn,
+    lengths_ref, offsets_ref, group_ref, blocks_ref, tokens_ref, prompt_ref,
+    wq_ref, wk_ref, wv_ref, wo_ref, gain_ref, q_gain_ref, k_gain_ref, turn_ref,
+    q_ref, pairs_ref, residual_ref, prefix_ref, meta_ref, info_ref, gout_ref,
+    x_ref, win_ref, wout_ref, rows, theirs, gin, stage, scaled, sums, squares, turn,
     a_send, a_recv, in_send, in_recv, out_send, out_recv, t_send, t_recv, p_send, p_recv, local_sem,
 ):
     x, y, z, core = place()
@@ -233,13 +297,29 @@
     above, below = step(y, 1), step(y, -1)
     row_count = residual_ref.shape[0]
     loads, at = [], 0
-    for n, ref in enumerate((tokens_ref, prompt_ref, marks_ref)):
+    for n, ref in enumerate((tokens_ref, prompt_ref)):
         loads.append(
             pltpu.make_async_copy(ref, x_ref.at[pl.ds(at, ref.shape[0])], local_sem.at[3 + n])
         )
         at += ref.shape[0]
     for load in loads:
         load.start()
+    slots = group_ref.shape[0]
+    lane = lax.broadcasted_iota(jnp.int32, (META, x_ref.shape[1]), 1)
+    marks = jnp.zeros(lane.shape, jnp.int32)
+    for j in range(slots):
+        marks = jnp.where(lane == j, group_ref[j], marks)
+        marks = jnp.where(lane == slots + j, blocks_ref[j], marks)
+    x_ref[at:] = marks.astype(jnp.float32).astype(jnp.bfloat16)
+    blocks, _, block_width = win_ref.shape
+    head = q_ref.shape[2]
+    wide = block_width - head
+    for n in range(blocks):
+        win_ref[n, :, :wide] = wq_ref[:, n * wide : (n + 1) * wide].astype(jnp.bfloat16)
+        column = n // 2 * head
+        narrow_ref = (wk_ref, wv_ref)[n % 2]
+        win_ref[n, :, wide:] = narrow_ref[:, column : column + head].astype(jnp.bfloat16)
+        wout_ref[n] = wo_ref[:, n * wide : n * wide + EARLY].astype(jnp.bfloat16)
     greet(column_peers() + plane_peers())
     inward_rows = Column(
         win_ref, lambda _, lo, at: stage.at[lo, at], a_send, a_recv, local_sem, 0
@@ -287,6 +367,11 @@
     @pl.when(away)
     def _():
         token_copy(8, mine, sibling, x_ref).start()
+
+    for tile in range(row_count // 64):
+        info_ref[tile * 64 : (tile + 1) * 64] = row_info(
+            tile * 64, 64, lengths_ref, offsets_ref, prompt_ref.shape[0], x, z
+        )
 
     def gin_viewer(owner):
         size = stage.shape[1] * stage.shape[2]
@@ -411,11 +496,10 @@
 
         multiply(2 + k)
 
-    meta_ref[...] = rows[count - META : count, 0:128]
-    meta = meta_ref[...].astype(jnp.float32)[0:1]
+    meta = rows[count - META : count, 0:128].astype(jnp.float32)
+    meta_ref[...] = meta.astype(jnp.int32)
+    meta = meta[0:1]
     half_heads = q_ref.shape[0] // 2
-    slots = 4.0
-    head = q_ref.shape[2]
     for tile in range(scaled.shape[0] // row_tile):
         span = slice(tile * row_tile, (tile + 1) * row_tile)
         scale = lax.rsqrt(squares[span] * (1.0 / (4 * width)) + epsilon)
@@ -442,10 +526,10 @@
             for h in range(2 * half_heads):
                 column = h % half_heads * head
                 q_ref[h, span] = turned(
-                    sums[h // half_heads, span, column : column + head], head_gain_ref[0:1]
+                    sums[h // half_heads, span, column : column + head], q_gain_ref[...]
                 )
         column = half_heads * head
-        pairs_ref[span, :head] = turned(sums[0, span, column : column + head], head_gain_ref[1:2])
+        pairs_ref[span, :head] = turned(sums[0, span, column : column + head], k_gain_ref[...])
         pairs_ref[span, head:] = (sums[1, span, column : column + head] * scale).astype(jnp.bfloat16)
 
     for act in later[4:]:
@@ -465,11 +549,14 @@
         token_copy(8, mine, sibling, x_ref).wait_send()
 
 
-def project(tokens, prompts, marks, win, wout, head, *tables):
+def project(lengths, offsets, group, blocks_of, tokens, prompts, wq, wk, wv, wo, *tables):
     row_count, width = tokens.shape
     used = row_count + prompts.shape[0]
     count = used + META
-    heads = 2 * (win.shape[2] // head - 1)
+    depth, head = wq.shape[0], tables[-1].shape[1]
+    blocks = 2 * wk.shape[1] // head
+    heads = 2 * wq.shape[1] // blocks // head
+    block_width = wq.shape[1] // blocks + head
     bf16 = jnp.bfloat16
     planes = [Plane.COPIES] * 4
     return pl.pallas_call(
@@ -480,35 +567,38 @@
             jax.ShapeDtypeStruct((used, 2 * head), bf16),
             jax.ShapeDtypeStruct((row_count, 2 * width), bf16),
             jax.ShapeDtypeStruct((row_count, 128), jnp.float32),
-            jax.ShapeDtypeStruct((META, 128), bf16),
-            jax.ShapeDtypeStruct((2, 2, 16, 4) + wout.shape[1:], bf16),
+            jax.ShapeDtypeStruct((META, 128), jnp.int32),
+            jax.ShapeDtypeStruct((row_count, 128), jnp.float32),
+            jax.ShapeDtypeStruct((2, 2, 16, 4, depth, EARLY), bf16),
         ),
-        in_specs=[ANY] * 5 + [VMEM] * len(tables),
-        out_specs=(VMEM,) * 5 + (ANY,),
+        in_specs=[SMEM] * 4 + [ANY] * 2 + [VMEM] * (4 + len(tables)),
+        out_specs=(VMEM,) * 6 + (ANY,),
         scratch_shapes=[
             pltpu.VMEM((count, width), bf16),
+            pltpu.VMEM((blocks, depth, block_width), bf16),
+            pltpu.VMEM((blocks, depth, EARLY), bf16),
             pltpu.VMEM((count, 4 * width), bf16),
             pltpu.VMEM((row_count, 2 * width), bf16),
-            pltpu.VMEM((2, 4 * width, win.shape[2]), bf16),
-            pltpu.VMEM((2, 4) + win.shape[1:], bf16),
+            pltpu.VMEM((2, 4 * width, block_width), bf16),
+            pltpu.VMEM((2, 4, depth, block_width), bf16),
             pltpu.VMEM((used, width), bf16),
-            pltpu.VMEM((2, used, win.shape[2]), jnp.float32),
+            pltpu.VMEM((2, used, block_width), jnp.float32),
             pltpu.VMEM((used, 128), jnp.float32),
             pltpu.VMEM((PBLOCKS, 2, used, head), jnp.float32),
         ]
         + [pltpu.SemaphoreType.DMA((n,)) for n in [14, 14] + planes + [13, 13, 2, 2, 6]],
         compiler_params=pltpu.CompilerParams(
-            collective_id=0, has_side_effects=True, vmem_limit_bytes=58 * 2**20
+            collective_id=0, has_side_effects=True, vmem_limit_bytes=60 * 2**20
         ),
-    )(tokens, prompts, marks, win, wout, *tables)
+    )(lengths, offsets, group, blocks_of, tokens, prompts, wq, wk, wv, wo, *tables)
 
 
 TILE = 64
 
 
 def attend_kernel(
-    q_hbm, pairs_hbm, info_hbm, prefix_hbm, group_ref, wout_ref, out_ref, gout_ref,
-    q_ref, pairs_ref, bounds_ref, prefix_ref, mine_ref, theirs_ref,
+    q_hbm, pairs_hbm, info_hbm, prefix_hbm, group_ref, wo_ref, out_ref, gout_ref,
+    wout_ref, q_ref, pairs_ref, bounds_ref, prefix_ref, mine_ref, theirs_ref,
     prompts, shared, total, sums, x_send, x_recv, load_sem, a_send, a_recv, out_send, out_recv, kv_send, kv_recv, local_sem,
 ):
     x, y, z, core = place()
@@ -524,6 +614,10 @@
     own_ref = pairs_ref.at[pl.ds(0, row_count)]
     prompt_ref = pairs_ref.at[pl.ds(row_count, prompts.shape[1])]
     sibling = device_at(x, y, z, 1 - core)
+    blocks = wout_ref.shape[0]
+    wide = wo_ref.shape[1] // blocks
+    for n in range(blocks):
+        wout_ref[n] = wo_ref[:, n * wide + EARLY : (n + 1) * wide].astype(jnp.bfloat16)
     greet(column_peers() + plane_peers())
     for load in loads:
         load.wait()
@@ -607,8 +701,8 @@
     for act in acts[3:]:
         act()
     kv.finish(prompt_viewer(1 - core))
-    for j in range(group_ref.shape[0]):
-        shared[j * prompts.shape[1] : (j + 1) * prompts.shape[1]] = prompts[group_ref[j]]
+    for j in range(shared.shape[0] // prompts.shape[1]):
+        shared[j * prompts.shape[1] : (j + 1) * prompts.shape[1]] = prompts[group_ref[0, j]]
     later = list(outward.rest())
     for tile in range(tiles):
         later[tile]()
@@ -628,21 +722,24 @@
     outward.finish(viewer(gout_ref, 1 - core))
 
 
-def attend(queries, pairs, info, prefix, group, wout):
+def attend(queries, pairs, info, prefix, meta, slots, wo):
     heads, count, head = queries.shape
     prompt = (pairs.shape[0] - count, pairs.shape[1])
     tiles = count // TILE
+    blocks = 2 * 4
+    late = (blocks, wo.shape[0], wo.shape[1] // blocks - EARLY)
     sems = [tiles, tiles, 4, 7, 7] + [Plane.COPIES] * 4 + [2]
     return pl.pallas_call(
         attend_kernel,
         name="attend",
         out_shape=(
             jax.ShapeDtypeStruct((count, heads * head), jnp.bfloat16),
-            jax.ShapeDtypeStruct((2, 2, 16, 4) + wout.shape[1:], wout.dtype),
+            jax.ShapeDtypeStruct((2, 2, 16, 4) + late[1:], jnp.bfloat16),
         ),
-        in_specs=[ANY] * 4 + [pl.BlockSpec(memory_space=pltpu.SMEM), ANY],
+        in_specs=[ANY] * 4 + [SMEM, VMEM],
         out_specs=(VMEM, ANY),
         scratch_shapes=[
+            pltpu.VMEM(late, jnp.bfloat16),
             pltpu.VMEM(queries.shape, queries.dtype),
             pltpu.VMEM(pairs.shape, pairs.dtype),
             pltpu.VMEM(info.shape, info.dtype),
@@ -650,46 +747,15 @@
             pltpu.VMEM((count, heads * head), jnp.bfloat16),
             pltpu.VMEM((count, heads * head), jnp.bfloat16),
             pltpu.VMEM((32,) + prompt, pairs.dtype),
-            pltpu.VMEM((group.shape[0] * prompt[0], prompt[1]), pairs.dtype),
+            pltpu.VMEM((slots * prompt[0], prompt[1]), pairs.dtype),
             pltpu.VMEM(queries.shape, jnp.float32),
             pltpu.VMEM(queries.shape, jnp.float32),
         ]
         + [pltpu.SemaphoreType.DMA((n,)) for n in sems],
         compiler_params=pltpu.CompilerParams(
-            collective_id=1, has_side_effects=True, vmem_limit_bytes=48 * 2**20
+            collective_id=1, has_side_effects=True, vmem_limit_bytes=60 * 2**20
         ),
-    )(queries, pairs, info, prefix, group, wout)
-
-
-BLOCK = 128
-LEVELS = ("z1", "x1", "z2", "x2")
-
-
-def level_bits(shift, sign):
-    odd = shift % 2 == 1
-    far = (shift >= 2) if sign == 1 else ((shift == 1) | (shift == 2))
-    return odd, far
-
-
-def along_z(shift, z):
-    return shift % 4, shift // 4 + (z < shift % 4).astype(jnp.int32)
-
-
-def y_shift(shift, x, z):
-    shift_z, need_x = along_z(shift, (z + shift) % 4)
-    end_x = (x + need_x) % 4
-    return (need_x // 4 + (end_x < need_x % 4).astype(jnp.int32)) % 2 == 1
-
-
-def move_masks(shift, x, z):
-    masks = []
-    for sign in (1, -1):
-        odd_z, far_z = level_bits(shift % 4, sign)
-        for level in LEVELS:
-            end_z = (z + (2 * far_z.astype(jnp.int32) if level in ("z1", "x1") else 0)) % 4
-            odd_x, far_x = level_bits(along_z(shift, end_z)[1] % 4, sign)
-            masks.append({"z1": odd_z, "x1": odd_x, "z2": far_z, "x2": far_x}[level])
-    return [mask.astype(jnp.float32) for mask in masks]
+    )(queries, pairs, info, prefix, meta, wo)
 
 
 def return_order(blocks):
@@ -928,21 +994,9 @@
         + [pltpu.SemaphoreType.DMA((n * blocks,)) for n in (4, 2, 3, levels, levels)]
         + [pltpu.SemaphoreType.DMA((6,))],
         compiler_params=pltpu.CompilerParams(
-            collective_id=2, has_side_effects=True, vmem_limit_bytes=56 * 2**20
+            collective_id=2, has_side_effects=True, vmem_limit_bytes=60 * 2**20
         ),
     )(blended, w0, w1, residual, info)
-
-
-def slot_layout(seq_lengths, row_count):
-    ends_at = jnp.cumsum(seq_lengths)
-    starts_at = ends_at - seq_lengths
-    position = jnp.arange(row_count, dtype=jnp.int32)
-    slot_of = jnp.sum((position[:, None] >= ends_at[None, :]).astype(jnp.int32), axis=1)
-    onehot = (
-        slot_of[:, None] == jnp.arange(seq_lengths.shape[0], dtype=jnp.int32)[None, :]
-    ).astype(jnp.int32)
-    within = position - jnp.sum(onehot * starts_at[None, :], axis=1)
-    return (slot_of, within, onehot)
 
 
 def shards(
@@ -960,51 +1014,19 @@
     prompt_blocks,
     dest_offset,
 ):
-    row_count, width = tokens.shape
-    prompt_len = prompt_rows.shape[0]
+    width = tokens.shape[1]
     head_size = q_gain.shape[0]
-    slot_count = seq_lengths.shape[0]
-    depth = w_query.shape[0]
-    groups = w_key.shape[1] // head_size
-    rep = lax.axis_index("rep")
-
-    halves = w_query.astype(jnp.bfloat16).reshape(depth, groups, 2, -1)
-    key_cols = w_key.astype(jnp.bfloat16).reshape(depth, groups, 1, head_size)
-    value_cols = w_value.astype(jnp.bfloat16).reshape(depth, groups, 1, head_size)
-    win = jnp.concatenate([halves, jnp.concatenate([key_cols, value_cols], axis=2)], axis=3)
-    win = win.transpose(1, 2, 0, 3).reshape(2 * groups, depth, -1)
-    wout = w_out.astype(jnp.bfloat16).reshape(2 * groups, -1, depth)
-    wout = [part.transpose(0, 2, 1) for part in (wout[:, :EARLY], wout[:, EARLY:])]
-    marks = jnp.concatenate([prompt_group, prompt_blocks]).astype(jnp.bfloat16)
-    marks = jnp.pad(marks[None, :], ((0, META - 1), (0, width - 2 * slot_count)))
-
-    plane_x, plane_z = rep // 4 % 4, rep % 4
-    slot_of, within, onehot = slot_layout(seq_lengths, row_count)
-    crosses = y_shift(dest_offset, plane_x, plane_z)
-    shift_rows = jnp.sum(onehot * dest_offset[None, :], axis=1)
-    row_crosses = jnp.sum(onehot * crosses[None, :], axis=1)
-    lanes = {
-        CROSS: row_crosses,
-        START: jnp.arange(row_count, dtype=jnp.int32) - within,
-        PROMPT: slot_of * prompt_len,
-        SLOT: slot_of,
-        WITHIN: within,
-    }
-    for n, mask in enumerate(move_masks(shift_rows, plane_x, plane_z)):
-        lanes[MOVES + n] = mask
-    lane = jnp.arange(128, dtype=jnp.int32)[None, :]
-    info = jnp.zeros((row_count, 128), jnp.float32)
-    for at, values in lanes.items():
-        info = jnp.where(lane == at, values.astype(jnp.float32)[:, None], info)
     spread = np.arange(head_size // 2, dtype=np.float32) * np.float32(2.0 / head_size)
     frequency = np.float32(rope_base) ** -spread
     frequency = jnp.asarray(np.tile(frequency.astype(np.float32), 2)[None, :])
-    queries, pairs, residual, prefix, meta, gout = project(
-        tokens, prompt_rows, marks, win, wout[0], head_size,
-        info, norm_gain[None, :], jnp.stack([q_gain, k_gain]), frequency,
+    outward = w_out.T
+    queries, pairs, residual, prefix, meta, info, gout = project(
+        seq_lengths, dest_offset, prompt_group, prompt_blocks, tokens, prompt_rows,
+        w_query, w_key, w_value, outward,
+        norm_gain[None, :], q_gain[None, :], k_gain[None, :], frequency,
     )
-    group_here = meta[0, :slot_count].astype(jnp.int32)
-    blended, gout_b = attend(queries, pairs, info, prefix, group_here, wout[1])
+    slots = seq_lengths.shape[0]
+    blended, gout_b = attend(queries, pairs, info, prefix, meta, slots, outward)
     features = 4 * width
     return return_rows(
         blended, gout.reshape(2, features, -1), gout_b.reshape(2, features, -1), residual, info

time: 237 us -> 223 us (0.941)
  the two profiles are of different devices: /device:TPU:16 before, /device:TPU:62 now
where the time goes in v4:
time: 223 us; the launch traced here: 222 us
  Pallas kernels  220 us (99%)
  local copies, waits for them, and re-layouts  2.34 us (1%)
    pallas_call x1, Pallas kernels, return_rows(): pl.pallas_call(return_kernel, name='return_rows', out_shape=jax.ShapeDtyp...  95.8 us
    pallas_call x1, Pallas kernels, project(): pl.pallas_call(project_kernel, name='project', out_shape=(jax.ShapeDtypeS...  81.7 us
    pallas_call x1, Pallas kernels, attend(): pl.pallas_call(attend_kernel, name='attend', out_shape=(jax.ShapeDtypeStr...  42.5 us

profile of v4, /device:TPU:62, one launch (start us, length us, event | category | flops | bytes accessed | tf_op | source)
XLA Modules:
  0.0 222.4 jit_solution(7087022851014263225)
XLA Ops:
  0.0 81.7 %project.1 = (bf16[8,448,128]{2,1,0:T(8,128)(2,1)}, bf16[576,256]{1,0:T(8,128)(2,1)}, bf16[448,2560]{1,0:T(8,128)(2,1)}, f32[448,128]{1,0:T(8,128)}, s32[16,128]...) custom-call(s32[4]{0:T(128)} %lengths_ref.1, s32[4]{0:T(128)} %offsets_ref.1, s32[4]{0:T(128)} %group_ref.1, ...), custom_call_target="tpu_custom_call" | custom-call | tf_op jit(solution)/shard_map/project/pallas_call | solution.py:562
  81.7 42.5 %attend.1 = (bf16[448,1024]{1,0:T(8,128)(2,1)}, bf16[2,2,16,4,40,256]{5,4,3,2,1,0:T(8,128)(2,1)}) custom-call(bf16[8,448,128]{2,1,0:T(8,128)(2,1)} %get-tuple-element.14.q_hbm, bf16[576,256]{1,0:T(8,128)(2,1)} %get-tuple-element.15.pairs_hbm, f32[448,128]{1,0:T(8,128)} %get-tuple-element.16.info_hbm.info_ref, f32[448,128]{1,0:T(8,128)} %get-tuple-element.17.prefix_hbm, ...), custom_call_target="tpu_custom_call" | custom-call | tf_op jit(solution)/shard_map/attend/pallas_call | solution.py:732
  124.3 95.8 %return_rows.1 = bf16[448,1280]{1,0:T(8,128)(2,1)} custom-call(bf16[448,1024]{1,0:T(8,128)(2,1)} %get-tuple-element.19.blend_hbm, bf16[2,5120,256]{2,1,0:T(8,128)(2,1)} %bitcast.6, bf16[2,5120,256]{2,1,0:T(8,128)(2,1)} %bitcast.7, bf16[448,2560]{1,0:T(8,128)(2,1)} %get-tuple-element.22.residual_hbm, f32[448,128]{1,0:T(8,128)} %get-tuple-element.16.info_hbm.info_ref), custom_call_target="tpu_custom_call" | custom-call | tf_op jit(solution)/shard_map/return_rows/pallas_call | solution.py:973
  220.1 2.3 %copy.16 = bf16[448,1280]{1,0:T(8,128)(2,1)} copy(bf16[448,1280]{1,0:T(8,128)(2,1)} %return_rows.1) | data formatting | bytes 2293760

commit v5 on v4

--- a/solution.py
+++ b/solution.py
@@ -683,23 +683,27 @@
         )
 
     tiles = q_ref.shape[1] // TILE
-    for tile in range(4):
-        own_tile(tile)
+    acts = list(kv.rest())
+    own_tile(0)
+    kv.first()
+    own_tile(1)
     rows.ready()
-    kv.first()
     outward.begin()
+    kv.opposite()
+    own_tile(2)
+    acts[0]()
+    own_tile(3)
+    for act in acts[1:3]:
+        act()
+    outward.first()
     own_tile(4)
-    kv.opposite()
-    own_tile(5)
-    kv.second(0)
-    outward.first()
-    own_tile(6)
-    acts = list(kv.rest())[1:]
-    for act in acts[:3]:
+    for act in acts[3:5]:
         act()
     outward.opposite()
-    for act in acts[3:]:
+    own_tile(5)
+    for act in acts[5:]:
         act()
+    own_tile(6)
     kv.finish(prompt_viewer(1 - core))
     for j in range(shared.shape[0] // prompts.shape[1]):
         shared[j * prompts.shape[1] : (j + 1) * prompts.shape[1]] = prompts[group_ref[0, j]]
@@ -759,7 +763,7 @@
 
 
 def return_order(blocks):
-    unit, seen, ahead, pace = 1.28, 1.6, 3.0, 8.2
+    unit, seen, ahead, pace = 1.5, 1.6, 3.0, 9.0
     cost = {"multiply": 1.6, "add": 0.5, "finish": 0.4, "take": 0.3}
     free, summed, order, now = {}, {}, [], 0.0
     waiting = [(max(0.0, pace * p - ahead), 0, ("multiply", p)) for p in range(blocks // 2)]

time: 223 us -> 223 us (level)
  the two profiles are of different devices: /device:TPU:62 before, /device:TPU:16 now
where the time goes in v5:
time: 223 us; the launch traced here: 222 us
  Pallas kernels  220 us (99%)
  local copies, waits for them, and re-layouts  2.34 us (1%)
    pallas_call x1, Pallas kernels, return_rows(): pl.pallas_call(return_kernel, name='return_rows', out_shape=jax.ShapeDtyp...  93.8 us
    pallas_call x1, Pallas kernels, project(): pl.pallas_call(project_kernel, name='project', out_shape=(jax.ShapeDtypeS...  84.9 us
    pallas_call x1, Pallas kernels, attend(): pl.pallas_call(attend_kernel, name='attend', out_shape=(jax.ShapeDtypeStr...  41.3 us

profile of v5, /device:TPU:16, one launch (start us, length us, event | category | flops | bytes accessed | tf_op | source)
XLA Modules:
  0.0 222.3 jit_solution(3024642288050169194)
XLA Ops:
  0.0 84.9 %project.1 = (bf16[8,448,128]{2,1,0:T(8,128)(2,1)}, bf16[576,256]{1,0:T(8,128)(2,1)}, bf16[448,2560]{1,0:T(8,128)(2,1)}, f32[448,128]{1,0:T(8,128)}, s32[16,128]...) custom-call(s32[4]{0:T(128)} %lengths_ref.1, s32[4]{0:T(128)} %offsets_ref.1, s32[4]{0:T(128)} %group_ref.1, ...), custom_call_target="tpu_custom_call" | custom-call | tf_op jit(solution)/shard_map/project/pallas_call | solution.py:562
  84.9 41.3 %attend.1 = (bf16[448,1024]{1,0:T(8,128)(2,1)}, bf16[2,2,16,4,40,256]{5,4,3,2,1,0:T(8,128)(2,1)}) custom-call(bf16[8,448,128]{2,1,0:T(8,128)(2,1)} %get-tuple-element.14.q_hbm, bf16[576,256]{1,0:T(8,128)(2,1)} %get-tuple-element.15.pairs_hbm, f32[448,128]{1,0:T(8,128)} %get-tuple-element.16.info_hbm.info_ref, f32[448,128]{1,0:T(8,128)} %get-tuple-element.17.prefix_hbm, ...), custom_call_target="tpu_custom_call" | custom-call | tf_op jit(solution)/shard_map/attend/pallas_call | solution.py:736
  126.2 93.8 %return_rows.1 = bf16[448,1280]{1,0:T(8,128)(2,1)} custom-call(bf16[448,1024]{1,0:T(8,128)(2,1)} %get-tuple-element.19.blend_hbm, bf16[2,5120,256]{2,1,0:T(8,128)(2,1)} %bitcast.6, bf16[2,5120,256]{2,1,0:T(8,128)(2,1)} %bitcast.7, bf16[448,2560]{1,0:T(8,128)(2,1)} %get-tuple-element.22.residual_hbm, f32[448,128]{1,0:T(8,128)} %get-tuple-element.16.info_hbm.info_ref), custom_call_target="tpu_custom_call" | custom-call | tf_op jit(solution)/shard_map/return_rows/pallas_call | solution.py:977
  220.0 2.3 %copy.16 = bf16[448,1280]{1,0:T(8,128)(2,1)} copy(bf16[448,1280]{1,0:T(8,128)(2,1)} %return_rows.1) | data formatting | bytes 2293760
